TPU v7x, 256 devices: a whole 4x4x8 slice. The times are simulated.
256 devices in a mesh: tm: 8 (over y, core), row: 4 (over x), col: 8 (over z).
Axes of the slice: x: 4, y: 4, z: 8, core: 2. Of those that a mesh axis runs over, the one named last changes fastest.
Arguments:
- frames_in: bfloat16 [32, 96, 256, 128], P('tm', 'row', 'col'), may hold values from -6 to 6
- kernel_base: bfloat16 [3, 3, 3, 128, 128], replicated, may hold values from -0.109375 to 0.109375
- kernel_down: bfloat16 [2, 2, 2, 128, 256], replicated, may hold values from -0.1875 to 0.1875
- kernel_top: bfloat16 [3, 3, 3, 256, 256], replicated, may hold values from -0.078125 to 0.078125
- cotangent: bfloat16 [16, 48, 128, 256], P('tm', 'row', 'col'), may hold values from -6 to 6
Outputs:
- features: bfloat16 [16, 48, 128, 256], P('tm', 'row', 'col')
- grad_frames: float32 [32, 96, 256, 128], P('tm', 'row', 'col')
- grad_base: float32 [27, 128, 128], P(None, 'col', ('tm', 'row'))
- grad_down: float32 [8, 256, 128], P(None, 'col', ('tm', 'row'))
- grad_top: float32 [27, 256, 256], P(None, 'col', ('tm', 'row'))
All inputs are finite; a program needn't handle non-finite values.
Results may differ from a plain program's by a relative error of at most 0.025.
Values may be sent and summed in bfloat16 or wider, within the bound.
A program may use at most 192 MiB of HBM per device.

v0:
```python
import functools
import math
from types import SimpleNamespace

import jax
import jax.numpy as jnp
from jax import lax
from jax.experimental import pallas as pl
from jax.experimental.pallas import tpu as pltpu
from jax.sharding import PartitionSpec as P

F32 = jnp.float32
BF = jnp.bfloat16
ROWS = 20
TOP = 14


def dot(a, b, ca=1, cb=0):
    return lax.dot_general(a, b, (((ca,), (cb,)), ((), ())), preferred_element_type=F32)


def iota(shape, dim):
    return lax.broadcasted_iota(jnp.int32, shape, dim)


def shift_cols(value, by):
    width = value.shape[1]
    rolled = pltpu.roll(value, by % width, 1)
    gap = 0 if by > 0 else width - 1
    return jnp.where(iota(value.shape, 1) == gap, 0.0, rolled)


def pick(parts):
    out = jnp.zeros((parts[0].shape[0], 8, parts[0].shape[2]), F32)
    row = iota(out.shape, 1)
    for t, part in enumerate(parts):
        out = jnp.where(row == t, jnp.broadcast_to(part, out.shape), out)
    return out


def logistic(s):
    return 1.0 / (1.0 + jnp.exp(-s))


def weave(first, second):
    first = first.reshape(16, 8, first.shape[1])
    second = second.reshape(16, 8, second.shape[1])
    low = iota(first.shape, 1) < 4
    even = jnp.where(low, first, pltpu.roll(second, 4, 1))
    odd = jnp.where(low, pltpu.roll(first, 4, 1), second)
    return even, odd


class Halo:
    def __init__(self, comm, body, cols, land, send, recv, frames, height, back, where):
        self.comm, self.body, self.cols, self.land = comm, body, cols, land
        self.send, self.recv, self.back = send, recv, back
        self.frames, self.height, self.where = frames, height, where
        self.own = 0 if back else 2
        self.copies = []

    def start(self):
        tm, row, col = self.where
        step = -1 if self.back else 1
        h, f, own, body = self.height, self.frames, self.own, self.body
        edge = 0 if self.back else own + f - 2
        into = f if self.back else 0
        jobs = []
        for dt in (0, step):
            first, count, put = (own, f, own) if dt == 0 else (edge, 2, into)
            kind = 0 if dt == 0 else 1
            for dh in (0, 1, -1):
                src_h, n, dst_h = {0: (1, h, 1), 1: (h, 1, 0), -1: (1, 1, h + 1)}[dh]
                if dt or dh:
                    jobs.append((kind, (dt, dh, 0),
                                 body.at[pl.ds(first, count), pl.ds(src_h, n)],
                                 body.at[pl.ds(put, count), pl.ds(dst_h, n)]))
                for dw in (1, -1):
                    side = 0 if dw == 1 else 1
                    jobs.append((2, (dt, dh, dw),
                                 self.cols.at[1 - side, pl.ds(src_h - 1, n)],
                                 self.land.at[side, kind, pl.ds(dst_h, n)]))
        if not self.comm:
            return
        for i, (kind, (dt, dh, dw), src, dst) in enumerate(jobs):
            copy = pltpu.make_async_remote_copy(
                src_ref=src, dst_ref=dst, send_sem=self.send.at[i], recv_sem=self.recv.at[i],
                device_id=((tm + dt + 8) % 8, (row + dh + 4) % 4, (col + dw + 8) % 8),
                device_id_type=pl.DeviceIdType.MESH,
            )
            copy.start()
            self.copies.append((kind, copy))

    def wait(self, kind):
        for k, copy in self.copies:
            if k == kind:
                copy.wait_recv()
        row = self.where[1]
        zero = jnp.zeros(self.body.shape[2:], BF)
        frames = range(self.own, self.own + self.frames)
        if kind == 1:
            first = self.frames if self.back else 0
            frames = range(first, first + 2)

            @pl.when(self.where[0] == (7 if self.back else 0))
            def _():
                for t in frames:
                    for r in range(self.height + 2):
                        self.body[t, r] = zero

        if kind < 2:
            @pl.when(row == 0)
            def _():
                for t in frames:
                    self.body[t, 0] = zero

            @pl.when(row == 3)
            def _():
                for t in frames:
                    self.body[t, self.height + 1] = zero

    def column(self, side):
        tm, row, col = self.where
        cur = self.land[side, 0]
        far = self.land[side, 1]
        shape = cur.shape
        at_t, at_h = iota(shape, 1), iota(shape, 0)
        out = col == (7 if side else 0)
        edge = tm == (7 if self.back else 0)
        if self.back:
            is_far = at_t >= self.frames
            far = pltpu.roll(far, self.frames, 1)
        else:
            is_far = at_t < 2
            far = pltpu.roll(far, 8 - (self.frames - 2), 1) if self.frames > 2 else far
            cur = pltpu.roll(cur, 2, 1)
        drop = ((at_h == 0) & (row == 0)) | ((at_h == shape[0] - 1) & (row == 3))
        drop = drop | out | (is_far & edge) | (at_t >= self.frames + 2)
        return jnp.where(drop, 0.0, jnp.where(is_far, far, cur))

    def done(self):
        for _, copy in self.copies:
            copy.wait_send()


class Reduce:
    def __init__(self, comm, s, job, r0, n, where):
        self.comm, self.s, self.job, self.r0, self.n = comm, s, job, r0, n
        tm, row, col = where
        self.y, self.core, self.x, self.z = tm // 2, tm % 2, row, col
        self.half = n // 2
        self.started = []
        self.pending = []
        self.slot = 0

    def put(self, src, dst, y, core, x, z):
        if not self.comm:
            return
        i = self.slot
        self.slot += 1
        copy = pltpu.make_async_remote_copy(
            src_ref=src, dst_ref=dst,
            send_sem=self.s.rs_send.at[self.job, i], recv_sem=self.s.rs_recv.at[self.job, i],
            device_id=(2 * y + core, x, z), device_id_type=pl.DeviceIdType.MESH,
        )
        copy.start()
        self.started.append(copy)
        self.pending.append(copy)

    def arrive(self):
        for copy in self.pending:
            copy.wait_recv()
        self.pending = []

    def a(self):
        return pl.ds(self.r0, self.half)

    def b(self):
        return pl.ds(self.r0 + self.half, self.half)

    def start(self):
        all_r = pl.ds(self.r0, self.n)
        self.put(self.s.terms.at[:, 1 - self.core, :, :, all_r],
                 self.s.c_land.at[:, :, :, all_r], self.y, 1 - self.core, self.x, self.z)

    def planes(self):
        s, y, x = self.s, self.y, self.x
        self.arrive()
        all_r = pl.ds(self.r0, self.n)

        def add(i, _):
            yy, x1, par = i // 4, (i % 4) // 2, i % 2
            s.u[yy, x1, par, all_r] = (
                s.terms[yy, self.core, x1, par, all_r].astype(F32)
                + s.c_land[yy, x1, par, all_r].astype(F32)
            ).astype(BF)
            return _

        lax.fori_loop(0, 16, add, 0)
        for d in (2, 1, 3):
            to = (y + d) % 4
            self.put(s.u.at[to, :, :, self.a()], s.da.at[d - 1, :, :, self.a()],
                     to, self.core, x, self.z)
            to = (x + d) % 4
            self.put(s.u.at[:, to // 2, to % 2, self.b()], s.db.at[d - 1, :, self.b()],
                     y, self.core, to, self.z)

    def lines(self):
        s, y, x = self.s, self.y, self.x
        self.arrive()

        def add(i, _):
            x1, par = i // 2, i % 2
            total = s.u[y, x1, par, self.a()].astype(F32)
            for d in range(3):
                total = total + s.da[d, x1, par, self.a()].astype(F32)
            s.va[x1, par, self.a()] = total.astype(BF)
            total = s.u[i, x // 2, x % 2, self.b()].astype(F32)
            for d in range(3):
                total = total + s.db[d, i, self.b()].astype(F32)
            s.vb[i, self.b()] = total.astype(BF)
            return _

        lax.fori_loop(0, 4, add, 0)
        for d in (2, 1, 3):
            to = (x + d) % 4
            self.put(s.va.at[to // 2, to % 2, self.a()], s.ea.at[d - 1, self.a()],
                     y, self.core, to, self.z)
            to = (y + d) % 4
            self.put(s.vb.at[to, self.b()], s.eb.at[d - 1, self.b()],
                     to, self.core, x, self.z)

    def depth(self):
        s, y, x = self.s, self.y, self.x
        self.arrive()
        first = s.va[x // 2, x % 2, self.a()].astype(F32)
        second = s.vb[y, self.b()].astype(F32)
        for d in range(3):
            first = first + s.ea[d, self.a()].astype(F32)
            second = second + s.eb[d, self.b()].astype(F32)
        rows = self.half * 16
        both = jnp.concatenate([first.reshape(rows, 256), second.reshape(rows, 256)], axis=0)
        if self.job == 0:
            wide = jnp.concatenate([both, jnp.zeros((32, 256), F32)], axis=0).T
            s.zs[0] = wide.astype(BF).reshape(8, 32, 256)
        else:
            down = jnp.concatenate([both[:32], jnp.zeros((96, 256), F32)], axis=0).T
            base = jnp.concatenate([both[32:], jnp.zeros((64, 256), F32)], axis=0).T
            s.zs[1, :, :, :128] = down.astype(BF).reshape(8, 32, 128)
            s.zs[1, :, :16, 128:] = base[:128].astype(BF).reshape(8, 16, 128)
            s.zs[1, :, 16:, 128:] = base[128:].astype(BF).reshape(8, 16, 128)
        for d in (4, 3, 5, 2, 6, 1, 7):
            to = (self.z + d) % 8
            self.put(s.zs.at[self.job, to], s.zr.at[self.job, d - 1], y, self.core, x, to)

    def finish(self, out):
        self.arrive()
        total = self.s.zs[self.job, self.z].astype(F32)
        if self.comm:
            for d in range(7):
                total = total + self.s.zr[self.job, d].astype(F32)
        out[self.job] = total

    def done(self):
        for copy in self.started:
            copy.wait_send()


def scratch_list():
    dma = pltpu.SemaphoreType.DMA
    return dict(
        xe=((6, 26, 32, 128), BF),
        ge=((6, 26, 32, 128), BF),
        wf=((9, 128, 384), BF),
        wb=((384, 1152), BF),
        kd=((1024, 256), BF),
        kt=((27, 256, 256), BF),
        cot=((384, 256), BF),
        pre=((4, 768, 128), F32),
        hg=((4, 12, 2, 32, 128), F32),
        hc=((2, 2, 2, 12, 2, 16, 128), BF),
        s3=((4, 768, 384), BF),
        colx=((2, 192, 1152), BF),
        hl=((2, 192, 128), F32),
        acc=((9, 128, 384), F32),
        xt=((3, 4, 14, 16, 256), BF),
        gt=((3, 4, 14, 16, 256), BF),
        acc_t=((384, 256), F32),
        grd=((384, 256), BF),
        px=((2, 24, 8, 128), F32),
        pg=((2, 24, 8, 128), F32),
        lx=((2, 2, 26, 8, 128), F32),
        lg=((2, 2, 26, 8, 128), F32),
        pxt=((2, 12, 8, 256), F32),
        pgt=((2, 12, 8, 256), F32),
        lxt=((2, 2, 14, 8, 256), F32),
        lgt=((2, 2, 14, 8, 256), F32),
        terms=((4, 2, 2, 2, ROWS, 16, 256), BF),
        c_land=((4, 2, 2, ROWS, 16, 256), BF),
        u=((4, 2, 2, ROWS, 16, 256), BF),
        da=((3, 2, 2, ROWS, 16, 256), BF),
        db=((3, 4, ROWS, 16, 256), BF),
        va=((2, 2, ROWS, 16, 256), BF),
        vb=((4, ROWS, 16, 256), BF),
        ea=((3, ROWS, 16, 256), BF),
        eb=((3, ROWS, 16, 256), BF),
        zs=((2, 8, 32, 256), BF),
        zr=((2, 7, 32, 256), BF),
        local=dma((8,)),
        h_send=dma((4, 17)),
        h_recv=dma((4, 17)),
        rs_send=dma((2, 20)),
        rs_recv=dma((2, 20)),
    )


def base_conv(src, t, weights, turned, chunk):
    width = 384

    def part(h0, n):
        lhs = jnp.concatenate(
            [src[t + a, pl.ds(h0 + b, n)].reshape(n * 32, 128) for a in range(3) for b in range(3)],
            axis=1,
        )
        y = dot(lhs, weights, 1, 1 if turned else 0).reshape(n, 32, width)
        return y[..., 128:256] + shift_cols(y[..., :128], 1) + shift_cols(y[..., 256:], -1)

    return part


def kernel(comm, skip, frames, kb, kd, kt, cot, feat, gf, zout, *refs):
    names = list(scratch_list())
    s = SimpleNamespace(**dict(zip(names, refs)))
    if comm:
        where = (lax.axis_index("tm"), lax.axis_index("row"), lax.axis_index("col"))
    else:
        where = (jnp.int32(0), jnp.int32(0), jnp.int32(0))
    tm, row, col = where
    loads = [
        pltpu.make_async_copy(frames, s.xe.at[pl.ds(2, 4), pl.ds(1, 24)], s.local.at[0]),
        pltpu.make_async_copy(kb.at[:, 0], s.wf.at[:, :, pl.ds(0, 128)], s.local.at[1]),
        pltpu.make_async_copy(kb.at[:, 1], s.wf.at[:, :, pl.ds(128, 128)], s.local.at[2]),
        pltpu.make_async_copy(kb.at[:, 2], s.wf.at[:, :, pl.ds(256, 128)], s.local.at[3]),
        pltpu.make_async_copy(kd, s.kd, s.local.at[4]),
        pltpu.make_async_copy(kt, s.kt, s.local.at[5]),
        pltpu.make_async_copy(cot, s.cot, s.local.at[6]),
    ]
    for load in loads:
        load.start()
    halo_x = Halo(comm, s.xe, s.px, s.lx, s.h_send.at[0], s.h_recv.at[0], 4, 24, False, where)
    halo_xt = Halo(comm, s.xt.at[1], s.pxt, s.lxt, s.h_send.at[1], s.h_recv.at[1], 2, 12, False, where)
    halo_gt = Halo(comm, s.gt.at[1], s.pgt, s.lgt, s.h_send.at[2], s.h_recv.at[2], 2, 12, True, where)
    halo_g = Halo(comm, s.ge, s.pg, s.lg, s.h_send.at[3], s.h_recv.at[3], 4, 24, True, where)
    rs_top = Reduce(comm, s, 0, 0, TOP, where)
    rs_low = Reduce(comm, s, 1, TOP, ROWS - TOP, where)

    if comm:
        barrier = pltpu.get_barrier_semaphore()
        near = [(a, b, c) for a in (0, 1, -1) for b in (0, 1, -1) for c in (0, 1, -1)][1:]
        far = [(2, 0, 0), (4, 0, 0), (6, 0, 0), (0, 2, 0)] + [(0, 0, d) for d in (2, 3, 4, 5, 6)]
        for dt, dh, dw in near + far:
            pl.semaphore_signal(
                barrier, inc=1,
                device_id=((tm + dt + 8) % 8, (row + dh + 4) % 4, (col + dw + 8) % 8),
                device_id_type=pl.DeviceIdType.MESH,
            )
    loads[0].wait()
    left, right = [], []
    for t in range(4):
        left.append(s.xe[2 + t, pl.ds(1, 24), pl.ds(0, 16)].astype(F32)[:, 0:1])
        right.append(s.xe[2 + t, pl.ds(1, 24), pl.ds(16, 16)].astype(F32)[:, 15:16])
    s.px[0] = pick(left)
    s.px[1] = pick(right)
    if comm:
        pl.semaphore_wait(barrier, len(near) + len(far))
    halo_x.start()

    for load in loads[1:4]:
        load.wait()
    for ab in range(9):
        for c in range(3):
            s.wb[c * 128:(c + 1) * 128, ab * 128:(ab + 1) * 128] = (
                s.wf[8 - ab, :, (2 - c) * 128:(3 - c) * 128])
    for load in loads[4:]:
        load.wait()

    weights = s.wf[...].reshape(1152, 384)

    def forward(i, _):
        t, h0 = i // 3, (i % 3) * 8
        value = base_conv(s.xe, t, s.wf[...].reshape(1152, 384), False, 8)(h0, 8)
        s.pre[t, pl.ds(pl.multiple_of(h0 * 32, 256), 256)] = value.reshape(256, 128)
        return _

    if "fwd" not in skip:
        halo_x.wait(0)
        lax.fori_loop(6, 12, forward, 0)
        halo_x.wait(1)
        lax.fori_loop(0, 6, forward, 0)
        halo_x.wait(2)
    for side in range(2):
        column = halo_x.column(side)
        pieces = []
        for a in range(3):
            moved = pltpu.roll(column, 8 - a, 1) if a else column
            for b in range(3):
                pieces.append(moved[b:b + 24].reshape(192, 128).astype(BF))
        lhs = jnp.concatenate(pieces, axis=1)
        s.colx[side] = lhs
        c = 2 * side
        s.hl[side] = dot(lhs, s.wf[:, :, c * 128:(c + 1) * 128].reshape(1152, 128))
    for t in range(4):
        for side in range(2):
            at = pl.ds(31 * side, 24, stride=32)
            s.pre[t, at] = s.pre[t, at] + s.hl[side, pl.ds(t, 24, stride=8)]

    def act(i, _):
        t, h1 = i // 12, i % 12
        rows = pl.ds(pl.multiple_of(h1 * 64, 64), 64)
        pre = s.pre[t, rows]
        q = logistic(pre)
        x = s.xe[2 + t, pl.ds(1 + 2 * h1, 2)].reshape(64, 128).astype(F32)
        hidden = (x + pre * q).astype(BF).astype(F32)
        s.hg[t, h1] = hidden.reshape(2, 32, 128)
        s.pre[t, rows] = q * (1.0 + pre * (1.0 - q))
        return _

    lax.fori_loop(0, 48, act, 0)
    for t in range(4):
        for c in range(2):
            s.hc[c, t // 2, t % 2] = s.hg[t, :, :, pl.ds(c, 16, stride=2), :].astype(BF)
    taps = [(a, b, c) for a in range(2) for b in range(2) for c in range(2)]
    lhs = jnp.concatenate([s.hc[c, :, a, :, b].reshape(384, 128) for a, b, c in taps], axis=1)
    reduced = dot(lhs, s.kd[...]).astype(BF)
    red32 = reduced.astype(F32).reshape(2, 12, 16, 256)
    s.xt[1, pl.ds(2, 2), pl.ds(1, 12)] = reduced.reshape(2, 12, 16, 256)
    for side, w in ((0, 0), (1, 15)):
        s.pxt[side] = pick([red32[t, :, w:w + 1] for t in range(2)])
    halo_xt.start()

    def sides(halo, ext):
        for side in range(2):
            column = halo.column(side)
            for t in range(4):
                body = ext[1, t].astype(F32)
                rolled = pltpu.roll(body, 15 if side else 1, 1)
                edge = jnp.broadcast_to(column[:, t:t + 1], body.shape)
                put = jnp.where(iota(body.shape, 1) == (15 if side else 0), edge, rolled)
                ext[2 * side, t] = put.astype(BF)

    for kind in range(3):
        halo_xt.wait(kind)
    sides(halo_xt, s.xt)

    def top_conv(ext, turned):
        s.acc_t[...] = jnp.zeros((384, 256), F32)

        def step(ab, _):
            a, b = ab // 3, ab % 3
            total = s.acc_t[...]
            for c in range(3):
                lhs = ext[c, pl.ds(a, 2), pl.ds(b, 12)].reshape(384, 256)
                if turned:
                    total = total + dot(lhs, s.kt[26 - (ab * 3 + c)], 1, 1)
                else:
                    total = total + dot(lhs, s.kt[ab * 3 + c])
            s.acc_t[...] = total
            return _

        lax.fori_loop(0, 9, step, 0)
        return s.acc_t[...]

    if "top" not in skip:
        top_conv(s.xt, False)
    pre_top = s.acc_t[...]
    q = logistic(pre_top)
    red = s.xt[1, pl.ds(2, 2), pl.ds(1, 12)].reshape(384, 256).astype(F32)
    feat[...] = (red + pre_top * q).astype(BF)
    up = s.cot[...].astype(F32)
    slope = (up * (q * (1.0 + pre_top * (1.0 - q)))).astype(BF)
    s.grd[...] = slope
    slope32 = slope.astype(F32).reshape(2, 12, 16, 256)
    s.gt[1, pl.ds(0, 2), pl.ds(1, 12)] = slope.reshape(2, 12, 16, 256)
    for side, w in ((0, 0), (1, 15)):
        s.pgt[side] = pick([slope32[t, :, w:w + 1] for t in range(2)])
    halo_gt.start()

    def top_tap(tap):
        a, b, c = tap // 9, (tap // 3) % 3, tap % 3
        window = s.xt[c, pl.ds(a, 2), pl.ds(b, 12)].reshape(384, 256)
        return dot(window, s.grd[...], 0, 0).reshape(32, 8, 256)

    def top_pair(r, _):
        both = jnp.concatenate([top_tap(2 * r), top_tap(2 * r + 1)], axis=1)
        s.terms[:, :, :, :, r] = both.astype(BF).reshape(4, 2, 2, 2, 16, 256)
        return _

    if "tgrad" not in skip:
        lax.fori_loop(0, 13, top_pair, 0)
    both = jnp.concatenate([top_tap(26), jnp.zeros((32, 8, 256), F32)], axis=1)
    s.terms[:, :, :, :, 13] = both.astype(BF).reshape(4, 2, 2, 2, 16, 256)
    rs_top.start()

    for kind in range(3):
        halo_gt.wait(kind)
    sides(halo_gt, s.gt)
    if "top" not in skip:
        top_conv(s.gt, True)
    grad_red = (s.cot[...].astype(F32) + s.acc_t[...]).astype(BF)
    s.grd[...] = grad_red
    spread = dot(grad_red, s.kd[...], 1, 1)
    for i, (a, b, c) in enumerate(taps):
        part = spread[:, i * 128:(i + 1) * 128].reshape(2, 12, 16, 128)
        for t in range(2):
            s.hg[2 * t + a, :, b, pl.ds(c, 16, stride=2), :] = part[t]

    low, high = [], []
    for t in range(4):
        gh = s.hg[t].reshape(24, 32, 128)
        slope = (gh * s.pre[t].reshape(24, 32, 128)).astype(BF)
        s.ge[t, pl.ds(1, 24)] = slope
        slope32 = slope.astype(F32)
        low.append(slope32[:, 0:1])
        high.append(slope32[:, 31:32])
        s.s3[t, :, 128:256] = slope.reshape(768, 128)
        s.s3[t, :, :128] = shift_cols(slope32, -1).astype(BF).reshape(768, 128)
        s.s3[t, :, 256:] = shift_cols(slope32, 1).astype(BF).reshape(768, 128)
    s.pg[0] = pick(low)
    s.pg[1] = pick(high)
    halo_g.start()
    rs_top.planes()

    def store_low(r, lanes, group):
        first, second = weave(group[0], group[1]), weave(group[2], group[3])
        for par in range(2):
            both = jnp.concatenate([first[par], second[par]], axis=1).astype(BF)
            s.terms[:, :, :, par, r, :, lanes] = both.reshape(4, 2, 2, 16, both.shape[2])

    for g in range(2):
        group = [
            dot(s.hc[c, :, a, :, b].reshape(384, 128), s.grd[...], 0, 0)
            for a, b, c in taps[4 * g:4 * g + 4]
        ]
        store_low(TOP + g, slice(0, 256), group)

    def base_tap(ab, _):
        a, b = ab // 3, ab % 3
        total = jnp.zeros((128, 384), F32)
        for t in range(4):
            window = s.xe[t + a, pl.ds(b, 24)].reshape(768, 128)
            total = total + dot(window, s.s3[t], 0, 0)
        s.acc[ab] = total
        return _

    if "bgrad" not in skip:
        lax.fori_loop(0, 9, base_tap, 0)
    for side in range(2):
        extra = dot(s.colx[side], s.pg[side].reshape(192, 128).astype(BF), 0, 0)
        lanes = slice(256 * side, 256 * side + 128)
        s.acc[:, :, lanes] = s.acc[:, :, lanes] + extra.reshape(9, 128, 128)
    for g in range(7):
        group = []
        for tap in range(4 * g, 4 * g + 4):
            if tap < 27:
                c = tap % 3
                group.append(s.acc[tap // 3, :, c * 128:(c + 1) * 128])
            else:
                group.append(jnp.zeros((128, 128), F32))
        store_low(TOP + 2 + g // 2, slice(128 * (g % 2), 128 * (g % 2) + 128), group)
    s.terms[:, :, :, :, ROWS - 1, :, 128:] = jnp.zeros((4, 2, 2, 2, 16, 128), BF)
    rs_low.start()
    rs_top.lines()

    for kind in range(3):
        halo_g.wait(kind)
    rs_low.planes()

    def backward(i, _):
        t, h0 = i // 3, (i % 3) * 8
        value = base_conv(s.ge, t, s.wb[...], True, 8)(h0, 8)
        gh = s.hg[t].reshape(24, 32, 128) if False else s.hg[t, pl.ds(h0 // 2, 4)].reshape(256, 128)
        gf[t, pl.ds(pl.multiple_of(h0 * 32, 256), 256)] = gh + value.reshape(256, 128)
        return _

    if "bwd" not in skip:
        lax.fori_loop(0, 6, backward, 0)
    rs_top.depth()
    rs_low.lines()
    if "bwd" not in skip:
        lax.fori_loop(6, 12, backward, 0)
    for side in range(2):
        column = halo_g.column(side)
        pieces = []
        for a in range(3):
            moved = pltpu.roll(column, 8 - a, 1) if a else column
            for b in range(3):
                pieces.append(moved[b:b + 24].reshape(192, 128).astype(BF))
        lhs = jnp.concatenate(pieces, axis=1)
        c = 2 * side
        s.hl[side] = dot(lhs, s.wb[c * 128:(c + 1) * 128, :], 1, 1)
    for t in range(4):
        for side in range(2):
            at = pl.ds(31 * side, 24, stride=32)
            gf[t, at] = gf[t, at] + s.hl[side, pl.ds(t, 24, stride=8)]
    rs_low.depth()
    rs_top.finish(zout)
    rs_low.finish(zout)
    for user in (halo_x, halo_xt, halo_gt, halo_g, rs_top, rs_low):
        user.done()


def call(comm, skip, *args):
    scratch = [pltpu.VMEM(*v) if isinstance(v, tuple) else v for v in scratch_list().values()]
    vmem = pl.BlockSpec(memory_space=pltpu.VMEM)
    params = dict(collective_id=0, has_side_effects=True) if comm else {}
    return pl.pallas_call(
        functools.partial(kernel, comm, skip),
        out_shape=(
            jax.ShapeDtypeStruct((384, 256), BF),
            jax.ShapeDtypeStruct((4, 768, 128), F32),
            jax.ShapeDtypeStruct((2, 32, 256), F32),
        ),
        in_specs=[pl.BlockSpec(memory_space=pl.ANY)] * 5,
        out_specs=(vmem, vmem, vmem),
        scratch_shapes=scratch,
        compiler_params=pltpu.CompilerParams(vmem_limit_bytes=60 * 1024 * 1024, **params),
        cost_estimate=pl.CostEstimate(flops=13 * 10**9, bytes_accessed=10**7, transcendentals=10**6),
    )(*args)


def unpack(zout, base_cells, top_cells):
    top = zout[0].reshape(32, 32, 8)[:, :27].transpose(1, 0, 2) / math.sqrt(top_cells)
    down = zout[1, :, :32].reshape(32, 8, 4).transpose(1, 0, 2) / math.sqrt(top_cells)
    base = zout[1, :, 128:192].reshape(2, 16, 4, 4, 4).transpose(2, 0, 3, 1, 4)
    base = base.reshape(32, 16, 4)[:27] / math.sqrt(base_cells)
    return base, down, top


def body(frames_in, kernel_base, kernel_down, kernel_top, cotangent, comm=True, skip=()):
    feat, gf, zout = call(
        comm, skip,
        frames_in,
        kernel_base.reshape(9, 3, 128, 128),
        kernel_down.reshape(1024, 256),
        kernel_top.reshape(27, 256, 256),
        cotangent.reshape(384, 256),
    )
    devices = 1
    if comm:
        devices = lax.axis_size("tm") * lax.axis_size("row") * lax.axis_size("col")
    base, down, top = unpack(zout, devices * 3072, devices * 384)
    return feat.reshape(2, 12, 16, 256), gf.reshape(4, 24, 32, 128), base, down, top


def solution(mesh):
    return jax.shard_map(
        body,
        mesh=mesh,
        in_specs=(P("tm", "row", "col", None), P(), P(), P(), P("tm", "row", "col", None)),
        out_specs=(
            P("tm", "row", "col", None),
            P("tm", "row", "col", None),
            P(None, "col", ("tm", "row")),
            P(None, "col", ("tm", "row")),
            P(None, "col", ("tm", "row")),
        ),
        check_vma=False,
    )
```

profile of v0, /device:TPU:2, one launch (start us, length us, event | category | flops | bytes accessed | tf_op | source)
XLA Modules:
  0.0 96.2 jit_solution(13653481567627537284)
XLA Ops:
  0.6 86.7 %shard_map.92 = (bf16[384,256]{1,0:T(8,128)(2,1)}, f32[4,768,128]{2,1,0:T(8,128)}, f32[2,32,256]{2,1,0:T(8,128)}) custom-call(bf16[4,24,32,128]{3,2,1,0:T(8,128)(2,1)} %frames.1, bf16[9,3,128,128]{3,2,1,0:T(8,128)(2,1)} %bitcast.23, bf16[1024,256]{1,0:T(8,128)(2,1)} %bitcast.24, bf16[27,256,256]{2,1,0:T(8,128)(2,1)} %bitcast.22, bf16[384,256]{1,0:T(8,128)(2,1)} %bitcast.25), custom_call_target="tpu_custom_call" | custom-call | flops 12999999488 | bytes 10000000 | tf_op jit(solution)/shard_map/pallas_call | solution.py:616
  87.3 0.7 slice_multiply_fusion.2
  88.0 0.7 copy.15
  88.7 0.7 slice.15
  89.4 0.8 slice.18
  90.2 0.1 copy.13
  90.3 0.1 reshape_squeeze.7
  90.4 0.7 copy.17
  91.1 0.1 copy.16
  91.2 0.7 fusion
  91.9 1.6 %copy.20 = bf16[2,12,16,256]{3,2,1,0:T(8,128)(2,1)} copy(bf16[2,12,16,256]{3,2,1,0:T(8,128)(2,1)} %bitcast.20) | data formatting | bytes 393216
  93.5 2.7 %copy.21 = f32[4,24,32,128]{3,2,1,0:T(8,128)} copy(f32[4,24,32,128]{3,2,1,0:T(8,128)} %bitcast.16) | data formatting | bytes 3145728
  (2 shorter events, 0.0 us)
where the time goes:
time: 96.5 us; the launch traced here: 96.2 us
  Pallas kernels  86.7 us (90%)
  local copies, waits for them, and re-layouts  7.45 us (8%)
  other arithmetic  1.39 us (1%)
    pallas_call x1, Pallas kernels, call(): pl.pallas_call(functools.partial(kernel, comm, skip), out_shape=(jax.Shap...  86.7 us
    unnamed x3, local copies, waits for them, and re-layouts  4.99 us

commit v1 on v0

--- a/solution.py
+++ b/solution.py
@@ -36,6 +36,23 @@
     for t, part in enumerate(parts):
         out = jnp.where(row == t, jnp.broadcast_to(part, out.shape), out)
     return out
+
+
+def pack(value):
+    h, _, c = value.shape
+    pairs = value.reshape(h // 2, 2, 8, c)
+    both = pairs[:, 0] + pltpu.roll(pairs[:, 1], 4, 1)
+    return both.reshape(h // 4, 16, c).astype(BF)
+
+
+def unpack_rows(groups, h):
+    g, _, c = groups.shape
+    pairs = groups.astype(F32).reshape(2 * g, 8, c)
+    low = iota(pairs.shape, 1) < 4
+    even = jnp.where(low, pairs, 0.0)
+    odd = jnp.where(low, pltpu.roll(pairs, 4, 1), 0.0)
+    rows = jnp.stack([even, odd], axis=1).reshape(4 * g, 8, c)
+    return rows[3:h + 5]
 
 
 def logistic(s):
@@ -75,11 +92,14 @@
                     jobs.append((kind, (dt, dh, 0),
                                  body.at[pl.ds(first, count), pl.ds(src_h, n)],
                                  body.at[pl.ds(put, count), pl.ds(dst_h, n)]))
+                g = h // 4
+                src_g, n_g, dst_g = {0: (0, g, 1), 1: (g - 1, 1, 0), -1: (0, 1, g + 1)}[dh]
                 for dw in (1, -1):
                     side = 0 if dw == 1 else 1
                     jobs.append((2, (dt, dh, dw),
-                                 self.cols.at[1 - side, pl.ds(src_h - 1, n)],
-                                 self.land.at[side, kind, pl.ds(dst_h, n)]))
+                                 self.cols.at[1 - side, pl.ds(src_g, n_g)],
+                                 self.land.at[side, kind, pl.ds(dst_g, n_g)]))
+        jobs.sort(key=lambda job: job[0])
         if not self.comm:
             return
         for i, (kind, (dt, dh, dw), src, dst) in enumerate(jobs):
@@ -121,8 +141,8 @@
 
     def column(self, side):
         tm, row, col = self.where
-        cur = self.land[side, 0]
-        far = self.land[side, 1]
+        cur = unpack_rows(self.land[side, 0], self.height)
+        far = unpack_rows(self.land[side, 1], self.height)
         shape = cur.shape
         at_t, at_h = iota(shape, 1), iota(shape, 0)
         out = col == (7 if side else 0)
@@ -178,8 +198,8 @@
     def b(self):
         return pl.ds(self.r0 + self.half, self.half)
 
-    def start(self):
-        all_r = pl.ds(self.r0, self.n)
+    def start(self, r0, n):
+        all_r = pl.ds(r0, n)
         self.put(self.s.terms.at[:, 1 - self.core, :, :, all_r],
                  self.s.c_land.at[:, :, :, all_r], self.y, 1 - self.core, self.x, self.z)
 
@@ -197,6 +217,31 @@
             return _
 
         lax.fori_loop(0, 16, add, 0)
+        if self.job == 0:
+            up, down, opp = (y + 1) % 4, (y + 3) % 4, (y + 2) % 4
+            east, west, over = (x + 1) % 4, (x + 3) % 4, (x + 2) % 4
+            p, q, p2, q2 = self.quarters()
+
+            def along_y(to, unit, r, land):
+                self.put(s.u.at[unit, :, :, r], s.da.at[land, :, :, r], to, self.core, x, self.z)
+
+            def along_x(to, unit, r, land):
+                self.put(s.u.at[:, unit // 2, unit % 2, r], s.db.at[land, :, r],
+                         y, self.core, to, self.z)
+
+            along_y(up, opp, p, 0)
+            along_y(down, opp, q, 0)
+            along_x(east, over, p2, 0)
+            along_x(west, over, q2, 0)
+            self.later, self.pending = [], self.pending
+            first = self.pending
+            self.pending = []
+            along_y(up, up, q, 1)
+            along_y(down, down, p, 1)
+            along_x(east, east, q2, 1)
+            along_x(west, west, p2, 1)
+            self.later, self.pending = self.pending, first
+            return
         for d in (2, 1, 3):
             to = (y + d) % 4
             self.put(s.u.at[to, :, :, self.a()], s.da.at[d - 1, :, :, self.a()],
@@ -205,6 +250,33 @@
             self.put(s.u.at[:, to // 2, to % 2, self.b()], s.db.at[d - 1, :, self.b()],
                      y, self.core, to, self.z)
 
+    def quarters(self):
+        r, n = self.r0, self.n // 4
+        return tuple(pl.ds(r + i * n, n) for i in range(4))
+
+    def relay(self):
+        s, y, x = self.s, self.y, self.x
+        self.arrive()
+        up, down, east, west = (y + 1) % 4, (y + 3) % 4, (x + 1) % 4, (x + 3) % 4
+        p, q, p2, q2 = self.quarters()
+
+        def add(i, _):
+            x1, par = i // 2, i % 2
+            for to, r in ((up, p), (down, q)):
+                s.g[0, x1, par, r] = (
+                    s.u[to, x1, par, r].astype(F32) + s.da[0, x1, par, r].astype(F32)).astype(BF)
+            for to, r in ((east, p2), (west, q2)):
+                s.g[1, x1, par, r] = (
+                    s.u[i, to // 2, to % 2, r].astype(F32) + s.db[0, i, r].astype(F32)).astype(BF)
+            return _
+
+        lax.fori_loop(0, 4, add, 0)
+        self.put(s.g.at[0, :, :, p], s.da.at[2, :, :, p], up, self.core, x, self.z)
+        self.put(s.g.at[0, :, :, q], s.da.at[2, :, :, q], down, self.core, x, self.z)
+        self.put(s.g.at[1, :, :, p2], s.dc.at[:, :, p2], y, self.core, east, self.z)
+        self.put(s.g.at[1, :, :, q2], s.dc.at[:, :, q2], y, self.core, west, self.z)
+        self.pending = self.pending + self.later
+
     def lines(self):
         s, y, x = self.s, self.y, self.x
         self.arrive()
@@ -212,12 +284,16 @@
         def add(i, _):
             x1, par = i // 2, i % 2
             total = s.u[y, x1, par, self.a()].astype(F32)
-            for d in range(3):
+            for d in range(1 if self.job == 0 else 0, 3):
                 total = total + s.da[d, x1, par, self.a()].astype(F32)
             s.va[x1, par, self.a()] = total.astype(BF)
             total = s.u[i, x // 2, x % 2, self.b()].astype(F32)
-            for d in range(3):
-                total = total + s.db[d, i, self.b()].astype(F32)
+            if self.job == 0:
+                total = total + s.db[1, i, self.b()].astype(F32)
+                total = total + s.dc[x1, par, self.b()].astype(F32)
+            else:
+                for d in range(3):
+                    total = total + s.db[d, i, self.b()].astype(F32)
             s.vb[i, self.b()] = total.astype(BF)
             return _
 
@@ -241,25 +317,49 @@
         rows = self.half * 16
         both = jnp.concatenate([first.reshape(rows, 256), second.reshape(rows, 256)], axis=0)
         if self.job == 0:
-            wide = jnp.concatenate([both, jnp.zeros((32, 256), F32)], axis=0).T
-            s.zs[0] = wide.astype(BF).reshape(8, 32, 256)
+            s.zs[...] = both.T.astype(BF).reshape(8, 32, 256)
+            src, dst = s.zs, s.zr
         else:
-            down = jnp.concatenate([both[:32], jnp.zeros((96, 256), F32)], axis=0).T
-            base = jnp.concatenate([both[32:], jnp.zeros((64, 256), F32)], axis=0).T
-            s.zs[1, :, :, :128] = down.astype(BF).reshape(8, 32, 128)
-            s.zs[1, :, :16, 128:] = base[:128].astype(BF).reshape(8, 16, 128)
-            s.zs[1, :, 16:, 128:] = base[128:].astype(BF).reshape(8, 16, 128)
+            base = jnp.concatenate([both, jnp.zeros((64, 256), F32)], axis=0).T
+            s.zs1[:, :16] = base[:128].astype(BF).reshape(8, 16, 128)
+            s.zs1[:, 16:] = base[128:].astype(BF).reshape(8, 16, 128)
+            src, dst = s.zs1, s.zr1
         for d in (4, 3, 5, 2, 6, 1, 7):
             to = (self.z + d) % 8
-            self.put(s.zs.at[self.job, to], s.zr.at[self.job, d - 1], y, self.core, x, to)
-
-    def finish(self, out):
+            self.put(src.at[to], dst.at[d - 1], y, self.core, x, to)
+
+    def total(self):
+        s = self.s
         self.arrive()
-        total = self.s.zs[self.job, self.z].astype(F32)
+        src, dst = (s.zs, s.zr) if self.job == 0 else (s.zs1, s.zr1)
+        total = src[self.z].astype(F32)
         if self.comm:
             for d in range(7):
-                total = total + self.s.zr[self.job, d].astype(F32)
-        out[self.job] = total
+                total = total + dst[d].astype(F32)
+        pad = jnp.zeros((96, total.shape[1]), F32)
+        return jnp.concatenate([total, pad], axis=0)
+
+    def finish_top(self, top, down, scale):
+        turned = self.total().T * scale
+        top[...] = turned[:216, :32].reshape(27, 8, 32)
+        for tap in range(8):
+            down[tap] = turned[224 + 4 * tap:228 + 4 * tap, :32]
+
+    def finish_base(self, out, scale):
+        s = self.s
+        s.fin[...] = self.total().T * scale
+        parts = []
+        low = iota((8, 128), 0) < 4
+        for k in range(4):
+            rows = s.fin[pl.ds(k, 16, stride=4), :]
+            beside = pltpu.roll(rows, 112, 1)
+            for j in range(2):
+                first, second = rows[8 * j:8 * j + 8], beside[8 * j:8 * j + 8]
+                parts.append(jnp.where(low, first, pltpu.roll(second, 4, 0)))
+                parts.append(jnp.where(low, pltpu.roll(first, 4, 0), second))
+        taps = jnp.concatenate(parts, axis=0).T[:16]
+        for k in range(4):
+            out[:, k, :] = (pltpu.roll(taps, 128 - 32 * k, 1) if k else taps)[:, :27]
 
     def done(self):
         for copy in self.started:
@@ -283,18 +383,21 @@
         colx=((2, 192, 1152), BF),
         hl=((2, 192, 128), F32),
         acc=((9, 128, 384), F32),
+        xf=((3, 128, 4608), BF),
+        hf=((8, 128, 384), BF),
         xt=((3, 4, 14, 16, 256), BF),
         gt=((3, 4, 14, 16, 256), BF),
         acc_t=((384, 256), F32),
         grd=((384, 256), BF),
-        px=((2, 24, 8, 128), F32),
-        pg=((2, 24, 8, 128), F32),
-        lx=((2, 2, 26, 8, 128), F32),
-        lg=((2, 2, 26, 8, 128), F32),
-        pxt=((2, 12, 8, 256), F32),
-        pgt=((2, 12, 8, 256), F32),
-        lxt=((2, 2, 14, 8, 256), F32),
-        lgt=((2, 2, 14, 8, 256), F32),
+        sg=((2, 192, 128), BF),
+        px=((2, 6, 16, 128), BF),
+        pg=((2, 6, 16, 128), BF),
+        lx=((2, 2, 8, 16, 128), BF),
+        lg=((2, 2, 8, 16, 128), BF),
+        pxt=((2, 3, 16, 256), BF),
+        pgt=((2, 3, 16, 256), BF),
+        lxt=((2, 2, 5, 16, 256), BF),
+        lgt=((2, 2, 5, 16, 256), BF),
         terms=((4, 2, 2, 2, ROWS, 16, 256), BF),
         c_land=((4, 2, 2, ROWS, 16, 256), BF),
         u=((4, 2, 2, ROWS, 16, 256), BF),
@@ -304,31 +407,35 @@
         vb=((4, ROWS, 16, 256), BF),
         ea=((3, ROWS, 16, 256), BF),
         eb=((3, ROWS, 16, 256), BF),
-        zs=((2, 8, 32, 256), BF),
-        zr=((2, 7, 32, 256), BF),
+        dc=((2, 2, ROWS, 16, 256), BF),
+        g=((2, 2, 2, ROWS, 16, 256), BF),
+        zs=((8, 32, 256), BF),
+        zr=((7, 32, 256), BF),
+        zs1=((8, 32, 128), BF),
+        zr1=((7, 32, 128), BF),
+        fin=((128, 128), F32),
         local=dma((8,)),
         h_send=dma((4, 17)),
         h_recv=dma((4, 17)),
-        rs_send=dma((2, 20)),
-        rs_recv=dma((2, 20)),
+        rs_send=dma((2, 28)),
+        rs_recv=dma((2, 28)),
     )
 
 
-def base_conv(src, t, weights, turned, chunk):
-    width = 384
-
-    def part(h0, n):
-        lhs = jnp.concatenate(
+def base_conv(src, parts, weights, turned):
+    blocks = []
+    for t, h0, n in parts:
+        blocks.append(jnp.concatenate(
             [src[t + a, pl.ds(h0 + b, n)].reshape(n * 32, 128) for a in range(3) for b in range(3)],
             axis=1,
-        )
-        y = dot(lhs, weights, 1, 1 if turned else 0).reshape(n, 32, width)
-        return y[..., 128:256] + shift_cols(y[..., :128], 1) + shift_cols(y[..., 256:], -1)
-
-    return part
-
-
-def kernel(comm, skip, frames, kb, kd, kt, cot, feat, gf, zout, *refs):
+        ))
+    lhs = jnp.concatenate(blocks, axis=0) if len(blocks) > 1 else blocks[0]
+    y = dot(lhs, weights, 1, 1 if turned else 0).reshape(-1, 32, 384)
+    y = y[..., 128:256] + shift_cols(y[..., :128], 1) + shift_cols(y[..., 256:], -1)
+    return y.reshape(-1, 128)
+
+
+def kernel(comm, skip, scales, frames, kb, kd, kt, cot, feat, gf, out_base, out_down, out_top, *refs):
     names = list(scratch_list())
     s = SimpleNamespace(**dict(zip(names, refs)))
     if comm:
@@ -351,8 +458,8 @@
     halo_xt = Halo(comm, s.xt.at[1], s.pxt, s.lxt, s.h_send.at[1], s.h_recv.at[1], 2, 12, False, where)
     halo_gt = Halo(comm, s.gt.at[1], s.pgt, s.lgt, s.h_send.at[2], s.h_recv.at[2], 2, 12, True, where)
     halo_g = Halo(comm, s.ge, s.pg, s.lg, s.h_send.at[3], s.h_recv.at[3], 4, 24, True, where)
-    rs_top = Reduce(comm, s, 0, 0, TOP, where)
-    rs_low = Reduce(comm, s, 1, TOP, ROWS - TOP, where)
+    rs_top = Reduce(comm, s, 0, 0, TOP + 2, where)
+    rs_low = Reduce(comm, s, 1, TOP + 2, ROWS - TOP - 2, where)
 
     if comm:
         barrier = pltpu.get_barrier_semaphore()
@@ -369,8 +476,8 @@
     for t in range(4):
         left.append(s.xe[2 + t, pl.ds(1, 24), pl.ds(0, 16)].astype(F32)[:, 0:1])
         right.append(s.xe[2 + t, pl.ds(1, 24), pl.ds(16, 16)].astype(F32)[:, 15:16])
-    s.px[0] = pick(left)
-    s.px[1] = pick(right)
+    s.px[0] = pack(pick(left))
+    s.px[1] = pack(pick(right))
     if comm:
         pl.semaphore_wait(barrier, len(near) + len(far))
     halo_x.start()
@@ -384,19 +491,21 @@
     for load in loads[4:]:
         load.wait()
 
-    weights = s.wf[...].reshape(1152, 384)
-
-    def forward(i, _):
-        t, h0 = i // 3, (i % 3) * 8
-        value = base_conv(s.xe, t, s.wf[...].reshape(1152, 384), False, 8)(h0, 8)
-        s.pre[t, pl.ds(pl.multiple_of(h0 * 32, 256), 256)] = value.reshape(256, 128)
-        return _
+    def forward(*parts):
+        value = base_conv(s.xe, parts, s.wf[...].reshape(1152, 384), False)
+        at = 0
+        for t, h0, n in parts:
+            s.pre[t, h0 * 32:(h0 + n) * 32] = value[at:at + n * 32]
+            at += n * 32
 
     if "fwd" not in skip:
+        forward((2, 8, 8), (3, 8, 8))
         halo_x.wait(0)
-        lax.fori_loop(6, 12, forward, 0)
+        forward((2, 0, 8), (2, 16, 8))
+        forward((3, 0, 8), (3, 16, 8))
         halo_x.wait(1)
-        lax.fori_loop(0, 6, forward, 0)
+        forward((0, 0, 24))
+        forward((1, 0, 24))
         halo_x.wait(2)
     for side in range(2):
         column = halo_x.column(side)
@@ -415,17 +524,17 @@
             s.pre[t, at] = s.pre[t, at] + s.hl[side, pl.ds(t, 24, stride=8)]
 
     def act(i, _):
-        t, h1 = i // 12, i % 12
-        rows = pl.ds(pl.multiple_of(h1 * 64, 64), 64)
+        t, h1 = i // 3, (i % 3) * 4
+        rows = pl.ds(pl.multiple_of(h1 * 64, 256), 256)
         pre = s.pre[t, rows]
         q = logistic(pre)
-        x = s.xe[2 + t, pl.ds(1 + 2 * h1, 2)].reshape(64, 128).astype(F32)
+        x = s.xe[2 + t, pl.ds(1 + 2 * h1, 8)].reshape(256, 128).astype(F32)
         hidden = (x + pre * q).astype(BF).astype(F32)
-        s.hg[t, h1] = hidden.reshape(2, 32, 128)
+        s.hg[t, pl.ds(h1, 4)] = hidden.reshape(4, 2, 32, 128)
         s.pre[t, rows] = q * (1.0 + pre * (1.0 - q))
         return _
 
-    lax.fori_loop(0, 48, act, 0)
+    lax.fori_loop(0, 12, act, 0)
     for t in range(4):
         for c in range(2):
             s.hc[c, t // 2, t % 2] = s.hg[t, :, :, pl.ds(c, 16, stride=2), :].astype(BF)
@@ -435,8 +544,14 @@
     red32 = reduced.astype(F32).reshape(2, 12, 16, 256)
     s.xt[1, pl.ds(2, 2), pl.ds(1, 12)] = reduced.reshape(2, 12, 16, 256)
     for side, w in ((0, 0), (1, 15)):
-        s.pxt[side] = pick([red32[t, :, w:w + 1] for t in range(2)])
+        s.pxt[side] = pack(pick([red32[t, :, w:w + 1] for t in range(2)]))
     halo_xt.start()
+
+    for f in range(6):
+        for b in range(3):
+            s.xf[b, :, f * 768:(f + 1) * 768] = s.xe[f, pl.ds(b, 24)].reshape(768, 128).T
+    for i, (a, b, c) in enumerate(taps):
+        s.hf[i] = s.hc[c, :, a, :, b].reshape(384, 128).T
 
     def sides(halo, ext):
         for side in range(2):
@@ -457,14 +572,13 @@
 
         def step(ab, _):
             a, b = ab // 3, ab % 3
-            total = s.acc_t[...]
-            for c in range(3):
-                lhs = ext[c, pl.ds(a, 2), pl.ds(b, 12)].reshape(384, 256)
-                if turned:
-                    total = total + dot(lhs, s.kt[26 - (ab * 3 + c)], 1, 1)
-                else:
-                    total = total + dot(lhs, s.kt[ab * 3 + c])
-            s.acc_t[...] = total
+            lhs = jnp.concatenate(
+                [ext[c, pl.ds(a, 2), pl.ds(b, 12)].reshape(384, 256) for c in range(3)], axis=1)
+            if turned:
+                rhs = jnp.concatenate([s.kt[26 - 3 * ab - c] for c in range(3)], axis=1)
+                s.acc_t[...] += dot(lhs, rhs, 1, 1)
+            else:
+                s.acc_t[...] += dot(lhs, s.kt[pl.ds(3 * ab, 3)].reshape(768, 256))
             return _
 
         lax.fori_loop(0, 9, step, 0)
@@ -482,24 +596,31 @@
     slope32 = slope.astype(F32).reshape(2, 12, 16, 256)
     s.gt[1, pl.ds(0, 2), pl.ds(1, 12)] = slope.reshape(2, 12, 16, 256)
     for side, w in ((0, 0), (1, 15)):
-        s.pgt[side] = pick([slope32[t, :, w:w + 1] for t in range(2)])
+        s.pgt[side] = pack(pick([slope32[t, :, w:w + 1] for t in range(2)]))
     halo_gt.start()
 
-    def top_tap(tap):
-        a, b, c = tap // 9, (tap // 3) % 3, tap % 3
-        window = s.xt[c, pl.ds(a, 2), pl.ds(b, 12)].reshape(384, 256)
-        return dot(window, s.grd[...], 0, 0).reshape(32, 8, 256)
-
-    def top_pair(r, _):
-        both = jnp.concatenate([top_tap(2 * r), top_tap(2 * r + 1)], axis=1)
+    def top_taps(abs_):
+        lhs = jnp.concatenate(
+            [s.xt[c, pl.ds(ab // 3, 2), pl.ds(ab % 3, 12)].reshape(384, 256)
+             for ab in abs_ for c in range(3)], axis=1)
+        return dot(lhs, s.grd[...], 0, 0).reshape(-1, 32, 8, 256)
+
+    def top_store(r, first, second):
+        both = jnp.concatenate([first, second], axis=1)
         s.terms[:, :, :, :, r] = both.astype(BF).reshape(4, 2, 2, 2, 16, 256)
+
+    def top_six(i, _):
+        group = top_taps([2 * i, 2 * i + 1])
+        for k in range(3):
+            top_store(3 * i + k, group[2 * k], group[2 * k + 1])
         return _
 
     if "tgrad" not in skip:
-        lax.fori_loop(0, 13, top_pair, 0)
-    both = jnp.concatenate([top_tap(26), jnp.zeros((32, 8, 256), F32)], axis=1)
-    s.terms[:, :, :, :, 13] = both.astype(BF).reshape(4, 2, 2, 2, 16, 256)
-    rs_top.start()
+        lax.fori_loop(0, 4, top_six, 0)
+    group = top_taps([8])
+    top_store(12, group[0], group[1])
+    top_store(13, group[2], jnp.zeros((32, 8, 256), F32))
+    rs_top.start(0, TOP)
 
     for kind in range(3):
         halo_gt.wait(kind)
@@ -508,6 +629,18 @@
         top_conv(s.gt, True)
     grad_red = (s.cot[...].astype(F32) + s.acc_t[...]).astype(BF)
     s.grd[...] = grad_red
+
+    def store_low(r, lanes, group):
+        first, second = weave(group[0], group[1]), weave(group[2], group[3])
+        for par in range(2):
+            both = jnp.concatenate([first[par], second[par]], axis=1).astype(BF)
+            s.terms[:, :, :, par, r, :, lanes] = both.reshape(4, 2, 2, 16, both.shape[2])
+
+    terms = dot(s.hf[...].reshape(1024, 384), s.grd[...]).reshape(8, 128, 256)
+    for g in range(2):
+        store_low(TOP + g, slice(0, 256), [terms[4 * g + i] for i in range(4)])
+    rs_top.start(TOP, 2)
+
     spread = dot(grad_red, s.kd[...], 1, 1)
     for i, (a, b, c) in enumerate(taps):
         part = spread[:, i * 128:(i + 1) * 128].reshape(2, 12, 16, 128)
@@ -525,37 +658,26 @@
         s.s3[t, :, 128:256] = slope.reshape(768, 128)
         s.s3[t, :, :128] = shift_cols(slope32, -1).astype(BF).reshape(768, 128)
         s.s3[t, :, 256:] = shift_cols(slope32, 1).astype(BF).reshape(768, 128)
-    s.pg[0] = pick(low)
-    s.pg[1] = pick(high)
+    for side, parts in enumerate((low, high)):
+        edge = pick(parts)
+        s.pg[side] = pack(edge)
+        s.sg[side] = edge.reshape(192, 128).astype(BF)
     halo_g.start()
     rs_top.planes()
 
-    def store_low(r, lanes, group):
-        first, second = weave(group[0], group[1]), weave(group[2], group[3])
-        for par in range(2):
-            both = jnp.concatenate([first[par], second[par]], axis=1).astype(BF)
-            s.terms[:, :, :, par, r, :, lanes] = both.reshape(4, 2, 2, 16, both.shape[2])
-
-    for g in range(2):
-        group = [
-            dot(s.hc[c, :, a, :, b].reshape(384, 128), s.grd[...], 0, 0)
-            for a, b, c in taps[4 * g:4 * g + 4]
-        ]
-        store_low(TOP + g, slice(0, 256), group)
-
-    def base_tap(ab, _):
-        a, b = ab // 3, ab % 3
-        total = jnp.zeros((128, 384), F32)
-        for t in range(4):
-            window = s.xe[t + a, pl.ds(b, 24)].reshape(768, 128)
-            total = total + dot(window, s.s3[t], 0, 0)
-        s.acc[ab] = total
-        return _
+    def base_taps(a):
+        lhs = s.xf[:, :, a * 768:a * 768 + 3072].reshape(384, 3072)
+        total = dot(lhs, s.s3[...].reshape(3072, 384))
+        s.acc[3 * a:3 * a + 3] = total.reshape(3, 128, 384)
 
     if "bgrad" not in skip:
-        lax.fori_loop(0, 9, base_tap, 0)
+        base_taps(0)
+    rs_top.relay()
+    if "bgrad" not in skip:
+        base_taps(1)
+        base_taps(2)
     for side in range(2):
-        extra = dot(s.colx[side], s.pg[side].reshape(192, 128).astype(BF), 0, 0)
+        extra = dot(s.colx[side], s.sg[side], 0, 0)
         lanes = slice(256 * side, 256 * side + 128)
         s.acc[:, :, lanes] = s.acc[:, :, lanes] + extra.reshape(9, 128, 128)
     for g in range(7):
@@ -568,26 +690,26 @@
                 group.append(jnp.zeros((128, 128), F32))
         store_low(TOP + 2 + g // 2, slice(128 * (g % 2), 128 * (g % 2) + 128), group)
     s.terms[:, :, :, :, ROWS - 1, :, 128:] = jnp.zeros((4, 2, 2, 2, 16, 128), BF)
-    rs_low.start()
-    rs_top.lines()
+    rs_low.start(TOP + 2, ROWS - TOP - 2)
+
+    def backward(t):
+        value = base_conv(s.ge, [(t, 0, 24)], s.wb[...], True)
+        gf[t] = s.hg[t].reshape(768, 128) + value
 
     for kind in range(3):
         halo_g.wait(kind)
+    if "bwd" not in skip:
+        backward(0)
+    rs_top.lines()
     rs_low.planes()
-
-    def backward(i, _):
-        t, h0 = i // 3, (i % 3) * 8
-        value = base_conv(s.ge, t, s.wb[...], True, 8)(h0, 8)
-        gh = s.hg[t].reshape(24, 32, 128) if False else s.hg[t, pl.ds(h0 // 2, 4)].reshape(256, 128)
-        gf[t, pl.ds(pl.multiple_of(h0 * 32, 256), 256)] = gh + value.reshape(256, 128)
-        return _
-
     if "bwd" not in skip:
-        lax.fori_loop(0, 6, backward, 0)
+        backward(1)
+        backward(2)
+    rs_low.lines()
     rs_top.depth()
-    rs_low.lines()
     if "bwd" not in skip:
-        lax.fori_loop(6, 12, backward, 0)
+        backward(3)
+    rs_low.depth()
     for side in range(2):
         column = halo_g.column(side)
         pieces = []
@@ -602,54 +724,86 @@
         for side in range(2):
             at = pl.ds(31 * side, 24, stride=32)
             gf[t, at] = gf[t, at] + s.hl[side, pl.ds(t, 24, stride=8)]
-    rs_low.depth()
-    rs_top.finish(zout)
-    rs_low.finish(zout)
+    rs_top.finish_top(out_top, out_down, scales[1])
+    rs_low.finish_base(out_base, scales[0])
     for user in (halo_x, halo_xt, halo_gt, halo_g, rs_top, rs_low):
         user.done()
 
 
-def call(comm, skip, *args):
+def call(comm, skip, scales, *args):
     scratch = [pltpu.VMEM(*v) if isinstance(v, tuple) else v for v in scratch_list().values()]
     vmem = pl.BlockSpec(memory_space=pltpu.VMEM)
     params = dict(collective_id=0, has_side_effects=True) if comm else {}
     return pl.pallas_call(
-        functools.partial(kernel, comm, skip),
+        functools.partial(kernel, comm, skip, scales),
         out_shape=(
             jax.ShapeDtypeStruct((384, 256), BF),
             jax.ShapeDtypeStruct((4, 768, 128), F32),
-            jax.ShapeDtypeStruct((2, 32, 256), F32),
+            jax.ShapeDtypeStruct((16, 4, 27), F32),
+            jax.ShapeDtypeStruct((8, 4, 32), F32),
+            jax.ShapeDtypeStruct((27, 8, 32), F32),
         ),
         in_specs=[pl.BlockSpec(memory_space=pl.ANY)] * 5,
-        out_specs=(vmem, vmem, vmem),
+        out_specs=(vmem,) * 5,
         scratch_shapes=scratch,
         compiler_params=pltpu.CompilerParams(vmem_limit_bytes=60 * 1024 * 1024, **params),
         cost_estimate=pl.CostEstimate(flops=13 * 10**9, bytes_accessed=10**7, transcendentals=10**6),
     )(*args)
 
 
-def unpack(zout, base_cells, top_cells):
-    top = zout[0].reshape(32, 32, 8)[:, :27].transpose(1, 0, 2) / math.sqrt(top_cells)
-    down = zout[1, :, :32].reshape(32, 8, 4).transpose(1, 0, 2) / math.sqrt(top_cells)
-    base = zout[1, :, 128:192].reshape(2, 16, 4, 4, 4).transpose(2, 0, 3, 1, 4)
-    base = base.reshape(32, 16, 4)[:27] / math.sqrt(base_cells)
-    return base, down, top
+def hand_over_kernel(*refs):
+    n = (len(refs) - 2) // 3
+    come, go = refs[-2:]
+    pieces = []
+    for src, dst, mid in zip(refs[:n], refs[n:2 * n], refs[2 * n:3 * n]):
+        if src.shape[0] == 4:
+            pieces += [(src.at[t], mid.at[t], dst.at[t]) for t in range(4)]
+        else:
+            pieces.append((src, mid, dst))
+    inward = [pltpu.make_async_copy(a, b, come.at[i]) for i, (a, b, c) in enumerate(pieces)]
+    outward = [pltpu.make_async_copy(b, c, go.at[i]) for i, (a, b, c) in enumerate(pieces)]
+    for copy in inward:
+        copy.start()
+    for copy, after in zip(inward, outward):
+        copy.wait()
+        after.start()
+    for copy in outward:
+        copy.wait()
+
+
+def hand_over(*arrays):
+    n = len(arrays) + 3
+    return pl.pallas_call(
+        hand_over_kernel,
+        out_shape=tuple(jax.ShapeDtypeStruct(a.shape, a.dtype) for a in arrays),
+        in_specs=[pl.BlockSpec(memory_space=pl.ANY)] * len(arrays),
+        out_specs=tuple(pl.BlockSpec(memory_space=pl.ANY) for _ in arrays),
+        scratch_shapes=[pltpu.VMEM(a.shape, a.dtype) for a in arrays]
+        + [pltpu.SemaphoreType.DMA((n,)), pltpu.SemaphoreType.DMA((n,))],
+    )(*arrays)
 
 
 def body(frames_in, kernel_base, kernel_down, kernel_top, cotangent, comm=True, skip=()):
-    feat, gf, zout = call(
-        comm, skip,
+    devices = 1
+    if comm:
+        devices = lax.axis_size("tm") * lax.axis_size("row") * lax.axis_size("col")
+    scales = (1.0 / math.sqrt(devices * 3072), 1.0 / math.sqrt(devices * 384))
+    feat, gf, base, down, top = call(
+        comm, skip, scales,
         frames_in,
         kernel_base.reshape(9, 3, 128, 128),
         kernel_down.reshape(1024, 256),
         kernel_top.reshape(27, 256, 256),
         cotangent.reshape(384, 256),
     )
-    devices = 1
-    if comm:
-        devices = lax.axis_size("tm") * lax.axis_size("row") * lax.axis_size("col")
-    base, down, top = unpack(zout, devices * 3072, devices * 384)
-    return feat.reshape(2, 12, 16, 256), gf.reshape(4, 24, 32, 128), base, down, top
+    gf, feat, base, down, top = hand_over(gf, feat, base, down, top)
+    return (
+        feat.reshape(2, 12, 16, 256),
+        gf.reshape(4, 24, 32, 128),
+        base.transpose(2, 0, 1),
+        down.transpose(0, 2, 1),
+        top.transpose(0, 2, 1),
+    )
 
 
 def solution(mesh):

time: 96.5 us -> 80.5 us (0.83)
  local copies, waits for them, and re-layouts: 7.45 us -> 0 us
  Pallas kernels: 86.7 us -> 79.3 us
  other arithmetic: 1.39 us -> 0 us
    pallas_call x1 -> x2, Pallas kernels: 86.7 us -> 79.3 us  [the longest x1 77 us: call(): pl.pallas_call(functools.partial(kernel, comm, skip, scales), out_shape=(...]
    unnamed x3 -> x0, local copies, waits for them, and re-layouts: 4.99 us -> none
    slice x4 -> x0, local copies, waits for them, and re-layouts: 1.65 us -> none  [the longest x2 0.86 us: unpack(): zout[0].reshape(32, 32, 8)[:, :27].transpose(1, 0, 2) / math.sqrt(top_cells)]
    div x3 -> x0, other arithmetic: 1.39 us -> none  [the longest x1 0.72 us: unpack(): zout[1, :, :32].reshape(32, 8, 4).transpose(1, 0, 2) / math.sqrt(top_cells)]
where the time goes in v1:
time: 80.5 us; the launch traced here: 80.1 us
  Pallas kernels  79.3 us (99%)
    pallas_call x1, Pallas kernels, call(): pl.pallas_call(functools.partial(kernel, comm, skip, scales), out_shape=(...  77 us
    pallas_call x1, Pallas kernels, hand_over(): pl.pallas_call(hand_over_kernel, out_shape=tuple((jax.ShapeDtypeStruct(a....  2.38 us

profile of v1, /device:TPU:2, one launch (start us, length us, event | category | flops | bytes accessed | tf_op | source)
XLA Modules:
  0.0 80.1 jit_solution(2073529826636803707)
XLA Ops:
  0.6 77.0 %shard_map.92 = (bf16[384,256]{1,0:T(8,128)(2,1)}, f32[4,768,128]{2,1,0:T(8,128)}, f32[16,4,27]{2,1,0:T(4,128)}, f32[8,4,32]{2,1,0:T(4,128)}, f32[27,8,32]{2,1,0:T(8,128)}) custom-call(bf16[4,24,32,128]{3,2,1,0:T(8,128)(2,1)} %frames.1, bf16[9,3,128,128]{3,2,1,0:T(8,128)(2,1)} %bitcast.11, bf16[1024,256]{1,0:T(8,128)(2,1)} %bitcast.12, ...), custom_call_target="tpu_custom_call" | custom-call | flops 12999999488 | bytes 10000000 | tf_op jit(solution)/shard_map/pallas_call | solution.py:737
  77.6 2.4 %shard_map.93 = (f32[4,768,128]{2,1,0:T(8,128)}, bf16[384,256]{1,0:T(8,128)(2,1)}, f32[16,4,27]{2,1,0:T(4,128)}, f32[8,4,32]{2,1,0:T(4,128)}, f32[27,8,32]{2,1,0:T(8,128)}) custom-call(f32[4,768,128]{2,1,0:T(8,128)} %get-tuple-element.15.refs_0_, bf16[384,256]{1,0:T(8,128)(2,1)} %get-tuple-element.16.refs_1_, f32[16,4,27]{2,1,0:T(4,128)} %get-tuple-element.17.refs_2_, ...), custom_call_target="tpu_custom_call" | custom-call | tf_op jit(solution)/shard_map/pallas_call | solution.py:776

commit v2 on v1

--- a/solution.py
+++ b/solution.py
@@ -164,16 +164,16 @@
 
 
 class Reduce:
-    def __init__(self, comm, s, job, r0, n, where):
+    def __init__(self, comm, s, job, r0, n, first, where):
         self.comm, self.s, self.job, self.r0, self.n = comm, s, job, r0, n
+        self.first = first
         tm, row, col = where
         self.y, self.core, self.x, self.z = tm // 2, tm % 2, row, col
-        self.half = n // 2
         self.started = []
-        self.pending = []
+        self.pending = {}
         self.slot = 0
 
-    def put(self, src, dst, y, core, x, z):
+    def put(self, key, src, dst, y, core, x, z):
         if not self.comm:
             return
         i = self.slot
@@ -185,108 +185,106 @@
         )
         copy.start()
         self.started.append(copy)
-        self.pending.append(copy)
-
-    def arrive(self):
-        for copy in self.pending:
+        self.pending.setdefault(key, []).append(copy)
+
+    def arrive(self, key):
+        for copy in self.pending.pop(key, []):
             copy.wait_recv()
-        self.pending = []
 
     def a(self):
-        return pl.ds(self.r0, self.half)
+        return pl.ds(self.r0, self.first)
 
     def b(self):
-        return pl.ds(self.r0 + self.half, self.half)
-
-    def start(self, r0, n):
-        all_r = pl.ds(r0, n)
-        self.put(self.s.terms.at[:, 1 - self.core, :, :, all_r],
-                 self.s.c_land.at[:, :, :, all_r], self.y, 1 - self.core, self.x, self.z)
-
-    def planes(self):
-        s, y, x = self.s, self.y, self.x
-        self.arrive()
-        all_r = pl.ds(self.r0, self.n)
+        return pl.ds(self.r0 + self.first, self.n - self.first)
+
+    def halves(self, part):
+        r0, n = (self.r0, self.first) if part == "a" else (self.r0 + self.first, self.n - self.first)
+        return pl.ds(r0, n // 2), pl.ds(r0 + n // 2, n // 2)
+
+    def start(self, key, r0, n):
+        r = pl.ds(r0, n)
+        self.put("core" + key, self.s.terms.at[:, 1 - self.core, :, :, r],
+                 self.s.c_land.at[:, :, :, r], self.y, 1 - self.core, self.x, self.z)
+
+    def fold(self, key, r):
+        s = self.s
+        self.arrive("core" + key)
 
         def add(i, _):
             yy, x1, par = i // 4, (i % 4) // 2, i % 2
-            s.u[yy, x1, par, all_r] = (
-                s.terms[yy, self.core, x1, par, all_r].astype(F32)
-                + s.c_land[yy, x1, par, all_r].astype(F32)
+            s.u[yy, x1, par, r] = (
+                s.terms[yy, self.core, x1, par, r].astype(F32) + s.c_land[yy, x1, par, r].astype(F32)
             ).astype(BF)
             return _
 
         lax.fori_loop(0, 16, add, 0)
-        if self.job == 0:
-            up, down, opp = (y + 1) % 4, (y + 3) % 4, (y + 2) % 4
-            east, west, over = (x + 1) % 4, (x + 3) % 4, (x + 2) % 4
-            p, q, p2, q2 = self.quarters()
-
-            def along_y(to, unit, r, land):
-                self.put(s.u.at[unit, :, :, r], s.da.at[land, :, :, r], to, self.core, x, self.z)
-
-            def along_x(to, unit, r, land):
-                self.put(s.u.at[:, unit // 2, unit % 2, r], s.db.at[land, :, r],
-                         y, self.core, to, self.z)
-
-            along_y(up, opp, p, 0)
-            along_y(down, opp, q, 0)
-            along_x(east, over, p2, 0)
-            along_x(west, over, q2, 0)
-            self.later, self.pending = [], self.pending
-            first = self.pending
-            self.pending = []
-            along_y(up, up, q, 1)
-            along_y(down, down, p, 1)
-            along_x(east, east, q2, 1)
-            along_x(west, west, p2, 1)
-            self.later, self.pending = self.pending, first
-            return
-        for d in (2, 1, 3):
-            to = (y + d) % 4
-            self.put(s.u.at[to, :, :, self.a()], s.da.at[d - 1, :, :, self.a()],
-                     to, self.core, x, self.z)
-            to = (x + d) % 4
-            self.put(s.u.at[:, to // 2, to % 2, self.b()], s.db.at[d - 1, :, self.b()],
-                     y, self.core, to, self.z)
-
-    def quarters(self):
-        r, n = self.r0, self.n // 4
-        return tuple(pl.ds(r + i * n, n) for i in range(4))
-
-    def relay(self):
+
+    def along(self, key, part, step, unit, r, land):
+        s = self.s
+        if part == "a":
+            to, unit = (self.y + step) % 4, (self.y + unit) % 4
+            self.put(key, s.u.at[unit, :, :, r], s.da.at[land, :, :, r],
+                     to, self.core, self.x, self.z)
+        else:
+            to, unit = (self.x + step) % 4, (self.x + unit) % 4
+            self.put(key, s.u.at[:, unit // 2, unit % 2, r], s.db.at[land, :, r],
+                     self.y, self.core, to, self.z)
+
+    def send(self, part):
+        self.fold(part, self.a() if part == "a" else self.b())
+        p, q = self.halves(part)
+        self.along("relay" + part, part, 1, 2, p, 0)
+        self.along("relay" + part, part, 3, 2, q, 0)
+        self.along("line" + part, part, 1, 1, q, 1)
+        self.along("line" + part, part, 3, 3, p, 1)
+
+    def relay(self, part):
         s, y, x = self.s, self.y, self.x
-        self.arrive()
-        up, down, east, west = (y + 1) % 4, (y + 3) % 4, (x + 1) % 4, (x + 3) % 4
-        p, q, p2, q2 = self.quarters()
+        self.arrive("relay" + part)
+        p, q = self.halves(part)
+        if part == "a":
+            up, down = (y + 1) % 4, (y + 3) % 4
+        else:
+            up, down = (x + 1) % 4, (x + 3) % 4
 
         def add(i, _):
             x1, par = i // 2, i % 2
             for to, r in ((up, p), (down, q)):
-                s.g[0, x1, par, r] = (
-                    s.u[to, x1, par, r].astype(F32) + s.da[0, x1, par, r].astype(F32)).astype(BF)
-            for to, r in ((east, p2), (west, q2)):
-                s.g[1, x1, par, r] = (
-                    s.u[i, to // 2, to % 2, r].astype(F32) + s.db[0, i, r].astype(F32)).astype(BF)
+                if part == "a":
+                    s.g[0, x1, par, r] = (
+                        s.u[to, x1, par, r].astype(F32) + s.da[0, x1, par, r].astype(F32)).astype(BF)
+                else:
+                    s.g[1, x1, par, r] = (
+                        s.u[i, to // 2, to % 2, r].astype(F32) + s.db[0, i, r].astype(F32)).astype(BF)
             return _
 
         lax.fori_loop(0, 4, add, 0)
-        self.put(s.g.at[0, :, :, p], s.da.at[2, :, :, p], up, self.core, x, self.z)
-        self.put(s.g.at[0, :, :, q], s.da.at[2, :, :, q], down, self.core, x, self.z)
-        self.put(s.g.at[1, :, :, p2], s.dc.at[:, :, p2], y, self.core, east, self.z)
-        self.put(s.g.at[1, :, :, q2], s.dc.at[:, :, q2], y, self.core, west, self.z)
-        self.pending = self.pending + self.later
-
-    def lines(self):
+        for to, r in ((up, p), (down, q)):
+            if part == "a":
+                self.put("linea", s.g.at[0, :, :, r], s.da.at[2, :, :, r],
+                         to, self.core, x, self.z)
+            else:
+                self.put("lineb", s.g.at[1, :, :, r], s.dc.at[:, :, r],
+                         y, self.core, to, self.z)
+
+    def planes(self):
+        for part in ("a", "b"):
+            self.fold(part, self.a() if part == "a" else self.b())
+            for d in (2, 1, 3):
+                self.along("line" + part, part, d, d, self.a() if part == "a" else self.b(), d - 1)
+
+    def lines(self, part):
         s, y, x = self.s, self.y, self.x
-        self.arrive()
+        self.arrive("line" + part)
 
         def add(i, _):
             x1, par = i // 2, i % 2
-            total = s.u[y, x1, par, self.a()].astype(F32)
-            for d in range(1 if self.job == 0 else 0, 3):
-                total = total + s.da[d, x1, par, self.a()].astype(F32)
-            s.va[x1, par, self.a()] = total.astype(BF)
+            if part == "a":
+                total = s.u[y, x1, par, self.a()].astype(F32)
+                for d in range(1 if self.job == 0 else 0, 3):
+                    total = total + s.da[d, x1, par, self.a()].astype(F32)
+                s.va[x1, par, self.a()] = total.astype(BF)
+                return _
             total = s.u[i, x // 2, x % 2, self.b()].astype(F32)
             if self.job == 0:
                 total = total + s.db[1, i, self.b()].astype(F32)
@@ -299,23 +297,24 @@
 
         lax.fori_loop(0, 4, add, 0)
         for d in (2, 1, 3):
-            to = (x + d) % 4
-            self.put(s.va.at[to // 2, to % 2, self.a()], s.ea.at[d - 1, self.a()],
-                     y, self.core, to, self.z)
-            to = (y + d) % 4
-            self.put(s.vb.at[to, self.b()], s.eb.at[d - 1, self.b()],
-                     to, self.core, x, self.z)
+            if part == "a":
+                to = (x + d) % 4
+                self.put("depth", s.va.at[to // 2, to % 2, self.a()], s.ea.at[d - 1, self.a()],
+                         y, self.core, to, self.z)
+            else:
+                to = (y + d) % 4
+                self.put("depth", s.vb.at[to, self.b()], s.eb.at[d - 1, self.b()],
+                         to, self.core, x, self.z)
 
     def depth(self):
         s, y, x = self.s, self.y, self.x
-        self.arrive()
+        self.arrive("depth")
         first = s.va[x // 2, x % 2, self.a()].astype(F32)
         second = s.vb[y, self.b()].astype(F32)
         for d in range(3):
             first = first + s.ea[d, self.a()].astype(F32)
             second = second + s.eb[d, self.b()].astype(F32)
-        rows = self.half * 16
-        both = jnp.concatenate([first.reshape(rows, 256), second.reshape(rows, 256)], axis=0)
+        both = jnp.concatenate([first.reshape(-1, 256), second.reshape(-1, 256)], axis=0)
         if self.job == 0:
             s.zs[...] = both.T.astype(BF).reshape(8, 32, 256)
             src, dst = s.zs, s.zr
@@ -326,11 +325,11 @@
             src, dst = s.zs1, s.zr1
         for d in (4, 3, 5, 2, 6, 1, 7):
             to = (self.z + d) % 8
-            self.put(src.at[to], dst.at[d - 1], y, self.core, x, to)
+            self.put("z", src.at[to], dst.at[d - 1], y, self.core, x, to)
 
     def total(self):
         s = self.s
-        self.arrive()
+        self.arrive("z")
         src, dst = (s.zs, s.zr) if self.job == 0 else (s.zs1, s.zr1)
         total = src[self.z].astype(F32)
         if self.comm:
@@ -414,6 +413,9 @@
         zs1=((8, 32, 128), BF),
         zr1=((7, 32, 128), BF),
         fin=((128, 128), F32),
+        gfs=((4, 768, 128), F32),
+        feats=((384, 256), BF),
+        leave=dma((5,)),
         local=dma((8,)),
         h_send=dma((4, 17)),
         h_recv=dma((4, 17)),
@@ -458,8 +460,8 @@
     halo_xt = Halo(comm, s.xt.at[1], s.pxt, s.lxt, s.h_send.at[1], s.h_recv.at[1], 2, 12, False, where)
     halo_gt = Halo(comm, s.gt.at[1], s.pgt, s.lgt, s.h_send.at[2], s.h_recv.at[2], 2, 12, True, where)
     halo_g = Halo(comm, s.ge, s.pg, s.lg, s.h_send.at[3], s.h_recv.at[3], 4, 24, True, where)
-    rs_top = Reduce(comm, s, 0, 0, TOP + 2, where)
-    rs_low = Reduce(comm, s, 1, TOP + 2, ROWS - TOP - 2, where)
+    rs_top = Reduce(comm, s, 0, 0, TOP + 2, 10, where)
+    rs_low = Reduce(comm, s, 1, TOP + 2, ROWS - TOP - 2, 2, where)
 
     if comm:
         barrier = pltpu.get_barrier_semaphore()
@@ -531,7 +533,6 @@
         x = s.xe[2 + t, pl.ds(1 + 2 * h1, 8)].reshape(256, 128).astype(F32)
         hidden = (x + pre * q).astype(BF).astype(F32)
         s.hg[t, pl.ds(h1, 4)] = hidden.reshape(4, 2, 32, 128)
-        s.pre[t, rows] = q * (1.0 + pre * (1.0 - q))
         return _
 
     lax.fori_loop(0, 12, act, 0)
@@ -547,6 +548,15 @@
         s.pxt[side] = pack(pick([red32[t, :, w:w + 1] for t in range(2)]))
     halo_xt.start()
 
+    def steep(i, _):
+        t, h1 = i // 3, (i % 3) * 4
+        rows = pl.ds(pl.multiple_of(h1 * 64, 256), 256)
+        pre = s.pre[t, rows]
+        q = logistic(pre)
+        s.pre[t, rows] = q * (1.0 + pre * (1.0 - q))
+        return _
+
+    lax.fori_loop(0, 12, steep, 0)
     for f in range(6):
         for b in range(3):
             s.xf[b, :, f * 768:(f + 1) * 768] = s.xe[f, pl.ds(b, 24)].reshape(768, 128).T
@@ -568,28 +578,25 @@
     sides(halo_xt, s.xt)
 
     def top_conv(ext, turned):
-        s.acc_t[...] = jnp.zeros((384, 256), F32)
-
-        def step(ab, _):
-            a, b = ab // 3, ab % 3
+        for t in range(2):
             lhs = jnp.concatenate(
-                [ext[c, pl.ds(a, 2), pl.ds(b, 12)].reshape(384, 256) for c in range(3)], axis=1)
+                [ext[c, a + t, b:b + 12].reshape(192, 256)
+                 for a in range(3) for b in range(3) for c in range(3)], axis=1)
             if turned:
-                rhs = jnp.concatenate([s.kt[26 - 3 * ab - c] for c in range(3)], axis=1)
-                s.acc_t[...] += dot(lhs, rhs, 1, 1)
+                rhs = jnp.concatenate([s.kt[26 - i] for i in range(27)], axis=1)
+                part = dot(lhs, rhs, 1, 1)
             else:
-                s.acc_t[...] += dot(lhs, s.kt[pl.ds(3 * ab, 3)].reshape(768, 256))
-            return _
-
-        lax.fori_loop(0, 9, step, 0)
-        return s.acc_t[...]
+                part = dot(lhs, s.kt[...].reshape(6912, 256))
+            s.acc_t[192 * t:192 * t + 192] = part
 
     if "top" not in skip:
         top_conv(s.xt, False)
     pre_top = s.acc_t[...]
     q = logistic(pre_top)
     red = s.xt[1, pl.ds(2, 2), pl.ds(1, 12)].reshape(384, 256).astype(F32)
-    feat[...] = (red + pre_top * q).astype(BF)
+    s.feats[...] = (red + pre_top * q).astype(BF)
+    leaving = [pltpu.make_async_copy(s.feats, feat, s.leave.at[4])]
+    leaving[0].start()
     up = s.cot[...].astype(F32)
     slope = (up * (q * (1.0 + pre_top * (1.0 - q)))).astype(BF)
     s.grd[...] = slope
@@ -617,16 +624,18 @@
 
     if "tgrad" not in skip:
         lax.fori_loop(0, 4, top_six, 0)
+    rs_top.start("a", 0, 10)
     group = top_taps([8])
     top_store(12, group[0], group[1])
     top_store(13, group[2], jnp.zeros((32, 8, 256), F32))
-    rs_top.start(0, TOP)
+    rs_top.start("b", 10, TOP - 10)
 
     for kind in range(3):
         halo_gt.wait(kind)
     sides(halo_gt, s.gt)
     if "top" not in skip:
         top_conv(s.gt, True)
+    rs_top.send("a")
     grad_red = (s.cot[...].astype(F32) + s.acc_t[...]).astype(BF)
     s.grd[...] = grad_red
 
@@ -639,7 +648,7 @@
     terms = dot(s.hf[...].reshape(1024, 384), s.grd[...]).reshape(8, 128, 256)
     for g in range(2):
         store_low(TOP + g, slice(0, 256), [terms[4 * g + i] for i in range(4)])
-    rs_top.start(TOP, 2)
+    rs_top.start("b", TOP, 2)
 
     spread = dot(grad_red, s.kd[...], 1, 1)
     for i, (a, b, c) in enumerate(taps):
@@ -663,7 +672,7 @@
         s.pg[side] = pack(edge)
         s.sg[side] = edge.reshape(192, 128).astype(BF)
     halo_g.start()
-    rs_top.planes()
+    rs_top.send("b")
 
     def base_taps(a):
         lhs = s.xf[:, :, a * 768:a * 768 + 3072].reshape(384, 3072)
@@ -672,10 +681,11 @@
 
     if "bgrad" not in skip:
         base_taps(0)
-    rs_top.relay()
+    rs_top.relay("a")
     if "bgrad" not in skip:
         base_taps(1)
         base_taps(2)
+    rs_top.relay("b")
     for side in range(2):
         extra = dot(s.colx[side], s.sg[side], 0, 0)
         lanes = slice(256 * side, 256 * side + 128)
@@ -690,26 +700,11 @@
                 group.append(jnp.zeros((128, 128), F32))
         store_low(TOP + 2 + g // 2, slice(128 * (g % 2), 128 * (g % 2) + 128), group)
     s.terms[:, :, :, :, ROWS - 1, :, 128:] = jnp.zeros((4, 2, 2, 2, 16, 128), BF)
-    rs_low.start(TOP + 2, ROWS - TOP - 2)
-
-    def backward(t):
-        value = base_conv(s.ge, [(t, 0, 24)], s.wb[...], True)
-        gf[t] = s.hg[t].reshape(768, 128) + value
+    rs_low.start("a", TOP + 2, ROWS - TOP - 2)
+    rs_top.lines("a")
 
     for kind in range(3):
         halo_g.wait(kind)
-    if "bwd" not in skip:
-        backward(0)
-    rs_top.lines()
-    rs_low.planes()
-    if "bwd" not in skip:
-        backward(1)
-        backward(2)
-    rs_low.lines()
-    rs_top.depth()
-    if "bwd" not in skip:
-        backward(3)
-    rs_low.depth()
     for side in range(2):
         column = halo_g.column(side)
         pieces = []
@@ -720,12 +715,31 @@
         lhs = jnp.concatenate(pieces, axis=1)
         c = 2 * side
         s.hl[side] = dot(lhs, s.wb[c * 128:(c + 1) * 128, :], 1, 1)
-    for t in range(4):
+
+    def backward(t):
+        value = base_conv(s.ge, [(t, 0, 24)], s.wb[...], True)
+        s.gfs[t] = s.hg[t].reshape(768, 128) + value
         for side in range(2):
             at = pl.ds(31 * side, 24, stride=32)
-            gf[t, at] = gf[t, at] + s.hl[side, pl.ds(t, 24, stride=8)]
+            s.gfs[t, at] = s.gfs[t, at] + s.hl[side, pl.ds(t, 24, stride=8)]
+        copy = pltpu.make_async_copy(s.gfs.at[t], gf.at[t], s.leave.at[t])
+        copy.start()
+        leaving.append(copy)
+
+    backward(0)
+    rs_low.planes()
+    rs_top.lines("b")
+    backward(1)
+    backward(2)
+    rs_low.lines("a")
+    rs_low.lines("b")
+    backward(3)
+    rs_top.depth()
+    rs_low.depth()
     rs_top.finish_top(out_top, out_down, scales[1])
     rs_low.finish_base(out_base, scales[0])
+    for copy in leaving:
+        copy.wait()
     for user in (halo_x, halo_xt, halo_gt, halo_g, rs_top, rs_low):
         user.done()
 
@@ -744,7 +758,7 @@
             jax.ShapeDtypeStruct((27, 8, 32), F32),
         ),
         in_specs=[pl.BlockSpec(memory_space=pl.ANY)] * 5,
-        out_specs=(vmem,) * 5,
+        out_specs=(pl.BlockSpec(memory_space=pl.ANY),) * 2 + (vmem,) * 3,
         scratch_shapes=scratch,
         compiler_params=pltpu.CompilerParams(vmem_limit_bytes=60 * 1024 * 1024, **params),
         cost_estimate=pl.CostEstimate(flops=13 * 10**9, bytes_accessed=10**7, transcendentals=10**6),

time: 80.5 us -> 75.9 us (0.943)
  Pallas kernels: 79.3 us -> 74.9 us
    pallas_call x1, Pallas kernels: 77 us -> 72.6 us  [call(): pl.pallas_call(functools.partial(kernel, comm, skip, scales), out_shape=(...]
where the time goes in v2:
time: 75.9 us; the launch traced here: 75.7 us
  Pallas kernels  74.9 us (99%)
  between operations  0.8 us (1%)
    pallas_call x1, Pallas kernels, call(): pl.pallas_call(functools.partial(kernel, comm, skip, scales), out_shape=(...  72.6 us
    pallas_call x1, Pallas kernels, hand_over(): pl.pallas_call(hand_over_kernel, out_shape=tuple((jax.ShapeDtypeStruct(a....  2.38 us

profile of v2, /device:TPU:2, one launch (start us, length us, event | category | flops | bytes accessed | tf_op | source)
XLA Modules:
  0.0 75.7 jit_solution(5130756266417946652)
XLA Ops:
  0.6 72.6 %shard_map.92 = (bf16[384,256]{1,0:T(8,128)(2,1)}, f32[4,768,128]{2,1,0:T(8,128)}, f32[16,4,27]{2,1,0:T(4,128)}, f32[8,4,32]{2,1,0:T(4,128)}, f32[27,8,32]{2,1,0:T(8,128)}) custom-call(bf16[4,24,32,128]{3,2,1,0:T(8,128)(2,1)} %frames.1, bf16[9,3,128,128]{3,2,1,0:T(8,128)(2,1)} %bitcast.11, bf16[1024,256]{1,0:T(8,128)(2,1)} %bitcast.12, ...), custom_call_target="tpu_custom_call" | custom-call | flops 12999999488 | bytes 10000000 | tf_op jit(solution)/shard_map/pallas_call | solution.py:751
  73.2 2.4 %shard_map.93 = (f32[4,768,128]{2,1,0:T(8,128)}, bf16[384,256]{1,0:T(8,128)(2,1)}, f32[16,4,27]{2,1,0:T(4,128)}, f32[8,4,32]{2,1,0:T(4,128)}, f32[27,8,32]{2,1,0:T(8,128)}) custom-call(f32[4,768,128]{2,1,0:T(8,128)} %get-tuple-element.15.refs_0_, bf16[384,256]{1,0:T(8,128)(2,1)} %get-tuple-element.16.refs_1_, f32[16,4,27]{2,1,0:T(4,128)} %get-tuple-element.17.refs_2_, ...), custom_call_target="tpu_custom_call" | custom-call | tf_op jit(solution)/shard_map/pallas_call | solution.py:790

commit v3 on v2

--- a/solution.py
+++ b/solution.py
@@ -217,7 +217,7 @@
             ).astype(BF)
             return _
 
-        lax.fori_loop(0, 16, add, 0)
+        lax.fori_loop(0, 16, add, 0, unroll=4 if self.job == 0 else 16)
 
     def along(self, key, part, step, unit, r, land):
         s = self.s
@@ -258,7 +258,7 @@
                         s.u[i, to // 2, to % 2, r].astype(F32) + s.db[0, i, r].astype(F32)).astype(BF)
             return _
 
-        lax.fori_loop(0, 4, add, 0)
+        lax.fori_loop(0, 4, add, 0, unroll=4)
         for to, r in ((up, p), (down, q)):
             if part == "a":
                 self.put("linea", s.g.at[0, :, :, r], s.da.at[2, :, :, r],
@@ -295,7 +295,7 @@
             s.vb[i, self.b()] = total.astype(BF)
             return _
 
-        lax.fori_loop(0, 4, add, 0)
+        lax.fori_loop(0, 4, add, 0, unroll=4)
         for d in (2, 1, 3):
             if part == "a":
                 to = (x + d) % 4
@@ -733,8 +733,8 @@
     backward(2)
     rs_low.lines("a")
     rs_low.lines("b")
+    rs_top.depth()
     backward(3)
-    rs_top.depth()
     rs_low.depth()
     rs_top.finish_top(out_top, out_down, scales[1])
     rs_low.finish_base(out_base, scales[0])

time: 75.9 us -> 75.1 us (0.989)
    pallas_call x1, Pallas kernels: 72.6 us -> 71.8 us  [call(): pl.pallas_call(functools.partial(kernel, comm, skip, scales), out_shape=(...]
where the time goes in v3:
time: 75.1 us; the launch traced here: 75 us
  Pallas kernels  74.2 us (99%)
  between operations  0.8 us (1%)
    pallas_call x1, Pallas kernels, call(): pl.pallas_call(functools.partial(kernel, comm, skip, scales), out_shape=(...  71.8 us
    pallas_call x1, Pallas kernels, hand_over(): pl.pallas_call(hand_over_kernel, out_shape=tuple((jax.ShapeDtypeStruct(a....  2.38 us

profile of v3, /device:TPU:2, one launch (start us, length us, event | category | flops | bytes accessed | tf_op | source)
XLA Modules:
  0.0 75.0 jit_solution(9935342379352232266)
XLA Ops:
  0.6 71.8 %shard_map.92 = (bf16[384,256]{1,0:T(8,128)(2,1)}, f32[4,768,128]{2,1,0:T(8,128)}, f32[16,4,27]{2,1,0:T(4,128)}, f32[8,4,32]{2,1,0:T(4,128)}, f32[27,8,32]{2,1,0:T(8,128)}) custom-call(bf16[4,24,32,128]{3,2,1,0:T(8,128)(2,1)} %frames.1, bf16[9,3,128,128]{3,2,1,0:T(8,128)(2,1)} %bitcast.11, bf16[1024,256]{1,0:T(8,128)(2,1)} %bitcast.12, ...), custom_call_target="tpu_custom_call" | custom-call | flops 12999999488 | bytes 10000000 | tf_op jit(solution)/shard_map/pallas_call | solution.py:751
  72.4 2.4 %shard_map.93 = (f32[4,768,128]{2,1,0:T(8,128)}, bf16[384,256]{1,0:T(8,128)(2,1)}, f32[16,4,27]{2,1,0:T(4,128)}, f32[8,4,32]{2,1,0:T(4,128)}, f32[27,8,32]{2,1,0:T(8,128)}) custom-call(f32[4,768,128]{2,1,0:T(8,128)} %get-tuple-element.15.refs_0_, bf16[384,256]{1,0:T(8,128)(2,1)} %get-tuple-element.16.refs_1_, f32[16,4,27]{2,1,0:T(4,128)} %get-tuple-element.17.refs_2_, ...), custom_call_target="tpu_custom_call" | custom-call | tf_op jit(solution)/shard_map/pallas_call | solution.py:790

commit v4 on v3

--- a/solution.py
+++ b/solution.py
@@ -267,11 +267,11 @@
                 self.put("lineb", s.g.at[1, :, :, r], s.dc.at[:, :, r],
                          y, self.core, to, self.z)
 
-    def planes(self):
-        for part in ("a", "b"):
-            self.fold(part, self.a() if part == "a" else self.b())
-            for d in (2, 1, 3):
-                self.along("line" + part, part, d, d, self.a() if part == "a" else self.b(), d - 1)
+    def planes(self, part):
+        groups = self.a() if part == "a" else self.b()
+        self.fold(part, groups)
+        for d in (2, 1, 3):
+            self.along("line" + part, part, d, d, groups, d - 1)
 
     def lines(self, part):
         s, y, x = self.s, self.y, self.x
@@ -679,28 +679,41 @@
         total = dot(lhs, s.s3[...].reshape(3072, 384))
         s.acc[3 * a:3 * a + 3] = total.reshape(3, 128, 384)
 
+    def base_sides(first, last):
+        for side in range(2):
+            extra = dot(s.colx[side, :, first * 128:last * 128], s.sg[side], 0, 0)
+            lanes = slice(256 * side, 256 * side + 128)
+            s.acc[first:last, :, lanes] = (
+                s.acc[first:last, :, lanes] + extra.reshape(last - first, 128, 128))
+
+    def base_groups(first, last):
+        for g in range(first, last):
+            group = []
+            for tap in range(4 * g, 4 * g + 4):
+                if tap < 27:
+                    c = tap % 3
+                    group.append(s.acc[tap // 3, :, c * 128:(c + 1) * 128])
+                else:
+                    group.append(jnp.zeros((128, 128), F32))
+            lanes = slice(128 * (g % 2), 128 * (g % 2) + 128)
+            store_low(TOP + 2 + g // 2, lanes, group)
+
     if "bgrad" not in skip:
         base_taps(0)
     rs_top.relay("a")
     if "bgrad" not in skip:
         base_taps(1)
+    base_sides(0, 6)
+    base_groups(0, 4)
+    rs_low.start("a", TOP + 2, 2)
+    if "bgrad" not in skip:
         base_taps(2)
     rs_top.relay("b")
-    for side in range(2):
-        extra = dot(s.colx[side], s.sg[side], 0, 0)
-        lanes = slice(256 * side, 256 * side + 128)
-        s.acc[:, :, lanes] = s.acc[:, :, lanes] + extra.reshape(9, 128, 128)
-    for g in range(7):
-        group = []
-        for tap in range(4 * g, 4 * g + 4):
-            if tap < 27:
-                c = tap % 3
-                group.append(s.acc[tap // 3, :, c * 128:(c + 1) * 128])
-            else:
-                group.append(jnp.zeros((128, 128), F32))
-        store_low(TOP + 2 + g // 2, slice(128 * (g % 2), 128 * (g % 2) + 128), group)
+    base_sides(6, 9)
+    base_groups(4, 7)
     s.terms[:, :, :, :, ROWS - 1, :, 128:] = jnp.zeros((4, 2, 2, 2, 16, 128), BF)
-    rs_low.start("a", TOP + 2, ROWS - TOP - 2)
+    rs_low.start("b", TOP + 4, 2)
+    rs_low.planes("a")
     rs_top.lines("a")
 
     for kind in range(3):
@@ -727,7 +740,7 @@
         leaving.append(copy)
 
     backward(0)
-    rs_low.planes()
+    rs_low.planes("b")
     rs_top.lines("b")
     backward(1)
     backward(2)

time: 75.1 us -> 76.5 us (1.019)
  Pallas kernels: 74.2 us -> 75.6 us
    pallas_call x1, Pallas kernels: 71.8 us -> 73.2 us  [call(): pl.pallas_call(functools.partial(kernel, comm, skip, scales), out_shape=(...]
where the time goes in v4:
time: 76.5 us; the launch traced here: 76.4 us
  Pallas kernels  75.6 us (99%)
  between operations  0.8 us (1%)
    pallas_call x1, Pallas kernels, call(): pl.pallas_call(functools.partial(kernel, comm, skip, scales), out_shape=(...  73.2 us
    pallas_call x1, Pallas kernels, hand_over(): pl.pallas_call(hand_over_kernel, out_shape=tuple((jax.ShapeDtypeStruct(a....  2.38 us

profile of v4, /device:TPU:2, one launch (start us, length us, event | category | flops | bytes accessed | tf_op | source)
XLA Modules:
  0.0 76.4 jit_solution(8921726396563335953)
XLA Ops:
  0.6 73.2 %shard_map.92 = (bf16[384,256]{1,0:T(8,128)(2,1)}, f32[4,768,128]{2,1,0:T(8,128)}, f32[16,4,27]{2,1,0:T(4,128)}, f32[8,4,32]{2,1,0:T(4,128)}, f32[27,8,32]{2,1,0:T(8,128)}) custom-call(bf16[4,24,32,128]{3,2,1,0:T(8,128)(2,1)} %frames.1, bf16[9,3,128,128]{3,2,1,0:T(8,128)(2,1)} %bitcast.11, bf16[1024,256]{1,0:T(8,128)(2,1)} %bitcast.12, ...), custom_call_target="tpu_custom_call" | custom-call | flops 12999999488 | bytes 10000000 | tf_op jit(solution)/shard_map/pallas_call | solution.py:764
  73.8 2.4 %shard_map.93 = (f32[4,768,128]{2,1,0:T(8,128)}, bf16[384,256]{1,0:T(8,128)(2,1)}, f32[16,4,27]{2,1,0:T(4,128)}, f32[8,4,32]{2,1,0:T(4,128)}, f32[27,8,32]{2,1,0:T(8,128)}) custom-call(f32[4,768,128]{2,1,0:T(8,128)} %get-tuple-element.15.refs_0_, bf16[384,256]{1,0:T(8,128)(2,1)} %get-tuple-element.16.refs_1_, f32[16,4,27]{2,1,0:T(4,128)} %get-tuple-element.17.refs_2_, ...), custom_call_target="tpu_custom_call" | custom-call | tf_op jit(solution)/shard_map/pallas_call | solution.py:803
